TPU v7x, 128 devices: a whole 4x4x4 slice. The times are simulated.
128 devices in a mesh: dp: 32 (over z, x_hi, y), seq: 4 (over x_lo, core).
Axes of the slice: x: 4 (x_hi: 2, x_lo: 2; x = x_hi * 2 + x_lo), y: 4, z: 4, core: 2. Of those that a mesh axis runs over, the one named last changes fastest.
Arguments:
- src_x: bfloat16 [32, 1024, 768], P('dp', 'seq'), may hold values from -6 to 6
- tgt_x: bfloat16 [32, 512, 768], P('dp', 'seq'), may hold values from -6 to 6
- out_cot: bfloat16 [32, 512, 768], P('dp', 'seq'), may hold values from -6 to 6
- src_seg: int32 [32, 1024], P('dp', 'seq'), may hold values from 0 to 3, as said below
- tgt_seg: int32 [32, 512], P('dp', 'seq'), may hold values from 0 to 3, as said below
- src_pad: int32 [32, 1024], P('dp', 'seq'), may hold values from 0 to 1, as said below
- tgt_pad: int32 [32, 512], P('dp', 'seq'), may hold values from 0 to 1, as said below
- enc_master: float32 [768, 6144], P(('dp', 'seq'))
- dec_master: float32 [768, 9216], P(('dp', 'seq'))
- down_master: float32 [3072, 1536], P(('dp', 'seq'))
- small_master: float32 [768, 31], P(('dp', 'seq'))
- enc_first: float32 [768, 6144], P(('dp', 'seq'))
- dec_first: float32 [768, 9216], P(('dp', 'seq'))
- down_first: float32 [3072, 1536], P(('dp', 'seq'))
- small_first: float32 [768, 31], P(('dp', 'seq'))
- enc_second: float32 [768, 6144], P(('dp', 'seq'))
- dec_second: float32 [768, 9216], P(('dp', 'seq'))
- down_second: float32 [3072, 1536], P(('dp', 'seq'))
- small_second: float32 [768, 31], P(('dp', 'seq'))
Outputs:
- dec_out: float32 [32, 512, 768], P('dp', 'seq')
- src_grad: float32 [32, 1024, 768], P('dp', 'seq')
- tgt_grad: float32 [32, 512, 768], P('dp', 'seq')
- grad_norm: float32 [], replicated
- enc_new: float32 [768, 6144], P(('dp', 'seq'))
- dec_new: float32 [768, 9216], P(('dp', 'seq'))
- down_new: float32 [3072, 1536], P(('dp', 'seq'))
- small_new: float32 [768, 31], P(('dp', 'seq'))
- enc_first_new: float32 [768, 6144], P(('dp', 'seq'))
- dec_first_new: float32 [768, 9216], P(('dp', 'seq'))
- down_first_new: float32 [3072, 1536], P(('dp', 'seq'))
- small_first_new: float32 [768, 31], P(('dp', 'seq'))
- enc_second_new: float32 [768, 6144], P(('dp', 'seq'))
- dec_second_new: float32 [768, 9216], P(('dp', 'seq'))
- down_second_new: float32 [3072, 1536], P(('dp', 'seq'))
- small_second_new: float32 [768, 31], P(('dp', 'seq'))
- small_grad: float32 [768, 31], P(('dp', 'seq'))
Inputs may be any that keep to these rules, and one draw needn't show every extreme that they name: `src_seg`: in every row the ids never fall and each of 0 to 3 names a run of positions; in a row, source id j and target id j are one document. `tgt_seg`: as for src_seg. `src_pad`: in every row the entries are 1 up to some position and 0 after it; the zeros lie in the row's last document, whose first position holds a 1. `tgt_pad`: as for src_pad.
All inputs are finite; a program needn't handle non-finite values.
Results may differ from a plain program's by a relative error of at most 0.02.
The roundings to bfloat16 on the way count: a program that leaves them out, or rounds other values in their place, can miss the bound.
Values may be sent and summed in bfloat16 or wider, within the bound.
No kernel may reach another device: no remote copies, remote signals or barrier semaphores. Data moves between devices by JAX's collectives and lax.ppermute only.
A program may use at most 256 MiB of HBM per device.

v0:
```python
import jax
import jax.numpy as jnp
from jax import lax
from jax.sharding import PartitionSpec as P

D = 768
HEADS = 12
HEAD = 64
STEP = 10


HIGHEST = lax.Precision.HIGHEST
NORM_EPS = 1e-05
MASKED = -1000000000.0
BETA_FIRST = 0.9
BETA_SECOND = 0.999
ADAM_EPS = 1e-08
RATE_MATRIX = 0.1
RATE_SMALL = 0.5
DECAY_RATE = 0.01
CLIP_LEVEL = 1.0


def layer_norm(inputs, scaling, offset):
    center = inputs - jnp.mean(inputs, axis=-1, keepdims=True)
    spread = jnp.mean(center * center, axis=-1, keepdims=True)
    return center * lax.rsqrt(spread + NORM_EPS) * scaling + offset


def norm_back(inputs, scaling, offset, gradient):
    unused, pull = jax.vjp(layer_norm, inputs, scaling, offset)
    return pull(gradient)


def gelu_exact(values):
    return jax.nn.gelu(values, approximate=False)


def project(left, weight):
    return jnp.dot(left, weight, preferred_element_type=jnp.float32)


def project_t(left, right):
    return jnp.einsum("rlk,rlm->km", left, right, preferred_element_type=jnp.float32)


def back_through(gradient, weight):
    return jnp.einsum("rlm,km->rlk", gradient, weight, preferred_element_type=jnp.float32)


def wide_t(left, right):
    return jnp.einsum("rlk,rlm->km", left.astype(jnp.float32), right, precision=HIGHEST)


def wide_back(gradient, weight):
    return jnp.einsum("rlm,km->rlk", gradient, weight.astype(jnp.float32), precision=HIGHEST)


def bias_sum(values):
    return jnp.sum(values, axis=(0, 1), dtype=jnp.float32)


def split_heads(values):
    return values.reshape(values.shape[0], values.shape[1], HEADS, HEAD)


def scores_of(query, keys, allowed):
    raw_scores = jnp.einsum(
        "rqhe,rkhe->rhqk", split_heads(query), split_heads(keys), preferred_element_type=jnp.float32
    ) * HEAD ** (-0.5)
    return jnp.where(allowed[:, None], raw_scores, MASKED)


def attend_fwd(query, keys, values, allowed):
    scores = scores_of(query, keys, allowed)
    top_score = jnp.max(scores, axis=-1, keepdims=True)
    expo = jnp.exp(scores - top_score)
    summed = jnp.sum(expo, axis=-1, keepdims=True)
    probs = (expo / summed).astype(jnp.bfloat16)
    mixed = jnp.einsum(
        "rhqk,rkhe->rqhe", probs, split_heads(values), preferred_element_type=jnp.float32
    )
    return (mixed.reshape(query.shape).astype(jnp.bfloat16), top_score + jnp.log(summed))


def attend_back(query, keys, values, allowed, log_total, grad_mixed):
    scores = scores_of(query, keys, allowed)
    probs = jnp.exp(scores - log_total)
    grad_heads = split_heads(grad_mixed)
    grad_values = jnp.einsum(
        "rhqk,rqhe->rkhe",
        probs.astype(jnp.bfloat16),
        grad_heads,
        preferred_element_type=jnp.float32,
    )
    grad_probs = jnp.einsum(
        "rqhe,rkhe->rhqk", grad_heads, split_heads(values), preferred_element_type=jnp.float32
    )
    grad_scores = (
        probs * (grad_probs - jnp.sum(probs * grad_probs, axis=-1, keepdims=True))
    ).astype(jnp.bfloat16)
    scale = HEAD ** (-0.5)
    grad_query = (
        jnp.einsum(
            "rhqk,rkhe->rqhe", grad_scores, split_heads(keys), preferred_element_type=jnp.float32
        )
        * scale
    )
    grad_keys = (
        jnp.einsum(
            "rhqk,rqhe->rkhe", grad_scores, split_heads(query), preferred_element_type=jnp.float32
        )
        * scale
    )
    return (
        grad_query.reshape(query.shape),
        grad_keys.reshape(keys.shape),
        grad_values.reshape(values.shape),
    )


def feed_fwd(resid, w_in, w_out, params, base):
    ffn_norm = layer_norm(resid, params[:, base], params[:, base + 1]).astype(jnp.bfloat16)
    bias_in = params[:, base + 3 : base + 7].T.reshape(-1)
    hidden = project(ffn_norm, w_in) + bias_in
    active = gelu_exact(hidden).astype(jnp.bfloat16)
    return (ffn_norm, hidden, active, resid + project(active, w_out) + params[:, base + 2])


def feed_back(resid, saved, w_in, w_out, params, base, gradient):
    ffn_norm, hidden, active = (saved[0], saved[1], saved[2])
    branch = gradient.astype(jnp.bfloat16)
    grad_wout = project_t(active, branch)
    grad_bout = bias_sum(branch)
    grad_active = back_through(branch, w_out)
    unused, pull = jax.vjp(gelu_exact, hidden)
    grad_hidden = pull(grad_active)[0].astype(jnp.bfloat16)
    grad_win = project_t(ffn_norm, grad_hidden)
    grad_bin = bias_sum(grad_hidden).reshape(4, -1).T
    grad_normed = back_through(grad_hidden, w_in)
    grad_resid, grad_gain, grad_shift = norm_back(
        resid, params[:, base], params[:, base + 1], grad_normed
    )
    columns = jnp.stack([grad_gain, grad_shift, grad_bout], axis=1)
    return (gradient + grad_resid, grad_win, grad_wout, columns, grad_bin)


def out_back(grad_resid, attended, weight):
    branch = grad_resid.astype(jnp.bfloat16)
    weight_grad = project_t(attended, branch)
    grad_att = back_through(branch, weight).astype(jnp.bfloat16)
    return (weight_grad, bias_sum(branch), grad_att)


def in_back(resid, normed, grad_proj, weight, params, column, grad_resid):
    weight_grad = project_t(normed, grad_proj)
    grad_normed = back_through(grad_proj, weight)
    grad_input, grad_gain, grad_shift = norm_back(
        resid, params[:, column], params[:, column + 1], grad_normed
    )
    return (grad_resid + grad_input, weight_grad, grad_gain, grad_shift)


def adam_step(master, first, second, gradient, factor, rate, decay):
    clipped = gradient * factor
    first_new = BETA_FIRST * first + (1 - BETA_FIRST) * clipped
    second_new = BETA_SECOND * second + (1 - BETA_SECOND) * clipped * clipped
    first_hat = first_new / (1 - BETA_FIRST**STEP)
    second_hat = second_new / (1 - BETA_SECOND**STEP)
    master_new = master - rate * (first_hat / (jnp.sqrt(second_hat) + ADAM_EPS) + decay * master)
    return (master_new, first_new, second_new)


def per_device(
    src_x,
    tgt_x,
    out_cot,
    src_seg,
    tgt_seg,
    src_pad,
    tgt_pad,
    enc_master,
    dec_master,
    down_master,
    small_master,
    enc_first,
    dec_first,
    down_first,
    small_first,
    enc_second,
    dec_second,
    down_second,
    small_second,
):
    enc_w, dec_w, down_w, small_w = (
        lax.all_gather(enc_master.astype(jnp.bfloat16), ("dp", "seq"), axis=0, tiled=True),
        lax.all_gather(dec_master.astype(jnp.bfloat16), ("dp", "seq"), axis=0, tiled=True),
        lax.all_gather(down_master.astype(jnp.bfloat16), ("dp", "seq"), axis=0, tiled=True),
        lax.all_gather(small_master.astype(jnp.bfloat16), ("dp", "seq"), axis=0, tiled=True),
    )
    params = small_w.astype(jnp.float32)
    src_ids, src_mask, tgt_ids, tgt_mask = (
        lax.all_gather(src_seg, "seq", axis=1, tiled=True),
        lax.all_gather(src_pad, "seq", axis=1, tiled=True),
        lax.all_gather(tgt_seg, "seq", axis=1, tiled=True),
        lax.all_gather(tgt_pad, "seq", axis=1, tiled=True),
    )
    tgt_len = tgt_x.shape[1]
    query_spot = lax.axis_index("seq") * tgt_len + jnp.arange(tgt_len, dtype=jnp.int32)
    key_spot = jnp.arange(tgt_ids.shape[1], dtype=jnp.int32)
    allow_enc = (src_seg[:, :, None] == src_ids[:, None, :]) & (src_mask[:, None, :] == 1)
    allow_self = (
        (tgt_seg[:, :, None] == tgt_ids[:, None, :])
        & (tgt_mask[:, None, :] == 1)
        & (key_spot[None, None, :] <= query_spot[None, :, None])
    )
    allow_cross = (tgt_seg[:, :, None] == src_ids[:, None, :]) & (src_mask[:, None, :] == 1)
    zero_bias = jnp.zeros((D,), jnp.float32)
    source = src_x.astype(jnp.float32)
    enc_norm = layer_norm(source, params[:, 0], params[:, 1]).astype(jnp.bfloat16)
    enc_qkv = (
        project(enc_norm, enc_w[:, : 3 * D])
        + jnp.concatenate([params[:, 2], zero_bias, params[:, 3]])
    ).astype(jnp.bfloat16)
    enc_query = enc_qkv[..., :D]
    enc_keys, enc_values = (
        lax.all_gather(enc_qkv[..., D : 2 * D], "seq", axis=1, tiled=True),
        lax.all_gather(enc_qkv[..., 2 * D :], "seq", axis=1, tiled=True),
    )
    enc_att, enc_lse = attend_fwd(enc_query, enc_keys, enc_values, allow_enc)
    enc_one = source + project(enc_att, enc_w[:, 3 * D : 4 * D]) + params[:, 4]
    enc_ffn = feed_fwd(enc_one, enc_w[:, 4 * D :], down_w[:, :D], params, 5)
    enc_two = enc_ffn[3]
    memory = layer_norm(enc_two, params[:, 12], params[:, 13]).astype(jnp.bfloat16)
    target = tgt_x.astype(jnp.float32)
    dec_norm = layer_norm(target, params[:, 14], params[:, 15]).astype(jnp.bfloat16)
    dec_qkv = (
        project(dec_norm, dec_w[:, : 3 * D])
        + jnp.concatenate([params[:, 16], zero_bias, params[:, 17]])
    ).astype(jnp.bfloat16)
    dec_query = dec_qkv[..., :D]
    dec_keys, dec_values = (
        lax.all_gather(dec_qkv[..., D : 2 * D], "seq", axis=1, tiled=True),
        lax.all_gather(dec_qkv[..., 2 * D :], "seq", axis=1, tiled=True),
    )
    self_att, self_lse = attend_fwd(dec_query, dec_keys, dec_values, allow_self)
    dec_one = target + project(self_att, dec_w[:, 3 * D : 4 * D]) + params[:, 18]
    cross_norm = layer_norm(dec_one, params[:, 19], params[:, 20]).astype(jnp.bfloat16)
    cross_query = (project(cross_norm, dec_w[:, 4 * D : 5 * D]) + params[:, 21]).astype(
        jnp.bfloat16
    )
    kv_bias = jnp.concatenate([zero_bias, params[:, 22]])
    memory_all = lax.all_gather(memory, "seq", axis=1, tiled=True)
    cross_kv = (project(memory_all, dec_w[:, 5 * D : 7 * D]) + kv_bias).astype(jnp.bfloat16)
    cross_keys, cross_values = (cross_kv[..., :D], cross_kv[..., D:])
    cross_att, cross_lse = attend_fwd(cross_query, cross_keys, cross_values, allow_cross)
    dec_two = dec_one + project(cross_att, dec_w[:, 7 * D : 8 * D]) + params[:, 23]
    dec_ffn = feed_fwd(dec_two, dec_w[:, 8 * D :], down_w[:, D:], params, 24)
    dec_out = dec_ffn[3]
    grad_top = out_cot.astype(jnp.float32)
    grad_two, dec_in_grad, dec_out_grad, dec_ffn_small, dec_bin_grad = feed_back(
        dec_two, dec_ffn, dec_w[:, 8 * D :], down_w[:, D:], params, 24, grad_top
    )
    co_grad, co_bias, cross_grad_att = out_back(grad_two, cross_att, dec_w[:, 7 * D : 8 * D])
    cross_gq, cross_gk, cross_gv = attend_back(
        cross_query, cross_keys, cross_values, allow_cross, cross_lse, cross_grad_att
    )
    partial_kv = jnp.concatenate([cross_gk, cross_gv], axis=-1)
    ckv_grad = wide_t(memory_all, partial_kv)
    cv_bias = bias_sum(partial_kv[..., D:])
    grad_memory = lax.psum_scatter(
        wide_back(partial_kv, dec_w[:, 5 * D : 7 * D]).astype(jnp.bfloat16),
        "seq",
        scatter_dimension=1,
        tiled=True,
    ).astype(jnp.float32)
    grad_memory = grad_memory.astype(jnp.bfloat16).astype(jnp.float32)
    cross_gq = cross_gq.astype(jnp.bfloat16)
    grad_one, cq_grad, cross_gain, cross_shift = in_back(
        dec_one, cross_norm, cross_gq, dec_w[:, 4 * D : 5 * D], params, 19, grad_two
    )
    cq_bias = bias_sum(cross_gq)
    so_grad, so_bias, self_grad_att = out_back(grad_one, self_att, dec_w[:, 3 * D : 4 * D])
    self_gq, self_gk, self_gv = attend_back(
        dec_query, dec_keys, dec_values, allow_self, self_lse, self_grad_att
    )
    self_gk, self_gv = (
        lax.psum_scatter(
            self_gk.astype(jnp.bfloat16), "seq", scatter_dimension=1, tiled=True
        ).astype(jnp.float32),
        lax.psum_scatter(
            self_gv.astype(jnp.bfloat16), "seq", scatter_dimension=1, tiled=True
        ).astype(jnp.float32),
    )
    self_qkv_grad = jnp.concatenate([self_gq, self_gk, self_gv], axis=-1).astype(jnp.bfloat16)
    tgt_grad, sqkv_grad, self_gain, self_shift = in_back(
        target, dec_norm, self_qkv_grad, dec_w[:, : 3 * D], params, 14, grad_one
    )
    dec_grad = jnp.concatenate(
        [sqkv_grad, so_grad, cq_grad, ckv_grad, co_grad, dec_in_grad], axis=1
    )
    dec_small = jnp.concatenate(
        [
            jnp.stack(
                [
                    self_gain,
                    self_shift,
                    bias_sum(self_qkv_grad[..., :D]),
                    bias_sum(self_qkv_grad[..., 2 * D :]),
                    so_bias,
                    cross_gain,
                    cross_shift,
                    cq_bias,
                    cv_bias,
                    co_bias,
                ],
                axis=1,
            ),
            dec_ffn_small,
            dec_bin_grad,
        ],
        axis=1,
    )
    enc_grad_two, final_gain, final_shift = norm_back(
        enc_two, params[:, 12], params[:, 13], grad_memory
    )
    enc_grad_one, enc_in_grad, enc_out_grad, enc_ffn_small, enc_bin_grad = feed_back(
        enc_one, enc_ffn, enc_w[:, 4 * D :], down_w[:, :D], params, 5, enc_grad_two
    )
    eo_grad, eo_bias, enc_grad_att = out_back(enc_grad_one, enc_att, enc_w[:, 3 * D : 4 * D])
    enc_gq, enc_gk, enc_gv = attend_back(
        enc_query, enc_keys, enc_values, allow_enc, enc_lse, enc_grad_att
    )
    enc_gk, enc_gv = (
        lax.psum_scatter(
            enc_gk.astype(jnp.bfloat16), "seq", scatter_dimension=1, tiled=True
        ).astype(jnp.float32),
        lax.psum_scatter(
            enc_gv.astype(jnp.bfloat16), "seq", scatter_dimension=1, tiled=True
        ).astype(jnp.float32),
    )
    enc_qkv_grad = jnp.concatenate([enc_gq, enc_gk, enc_gv], axis=-1).astype(jnp.bfloat16)
    src_grad, eqkv_grad, enc_gain, enc_shift = in_back(
        source, enc_norm, enc_qkv_grad, enc_w[:, : 3 * D], params, 0, enc_grad_one
    )
    enc_grad = jnp.concatenate([eqkv_grad, eo_grad, enc_in_grad], axis=1)
    enc_small = jnp.concatenate(
        [
            jnp.stack(
                [
                    enc_gain,
                    enc_shift,
                    bias_sum(enc_qkv_grad[..., :D]),
                    bias_sum(enc_qkv_grad[..., 2 * D :]),
                    eo_bias,
                ],
                axis=1,
            ),
            enc_ffn_small,
            enc_bin_grad,
            jnp.stack([final_gain, final_shift], axis=1),
        ],
        axis=1,
    )
    shards = (
        lax.psum_scatter(enc_grad, ("dp", "seq"), scatter_dimension=0, tiled=True),
        lax.psum_scatter(dec_grad, ("dp", "seq"), scatter_dimension=0, tiled=True),
        lax.psum_scatter(
            jnp.concatenate([enc_out_grad, dec_out_grad], axis=1),
            ("dp", "seq"),
            scatter_dimension=0,
            tiled=True,
        ),
        lax.psum_scatter(
            jnp.concatenate([enc_small, dec_small], axis=1),
            ("dp", "seq"),
            scatter_dimension=0,
            tiled=True,
        ),
    )
    squares = (
        jnp.sum(shards[0] * shards[0])
        + jnp.sum(shards[1] * shards[1])
        + jnp.sum(shards[2] * shards[2])
        + jnp.sum(shards[3] * shards[3])
    )
    grad_norm = jnp.sqrt(lax.psum(squares, ("dp", "seq")))
    factor = CLIP_LEVEL / jnp.maximum(grad_norm, CLIP_LEVEL)
    enc_all = adam_step(
        enc_master, enc_first, enc_second, shards[0], factor, RATE_MATRIX, DECAY_RATE
    )
    dec_all = adam_step(
        dec_master, dec_first, dec_second, shards[1], factor, RATE_MATRIX, DECAY_RATE
    )
    down_all = adam_step(
        down_master, down_first, down_second, shards[2], factor, RATE_MATRIX, DECAY_RATE
    )
    small_all = adam_step(
        small_master, small_first, small_second, shards[3], factor, RATE_SMALL, 0.0
    )
    return (
        dec_out,
        src_grad,
        tgt_grad,
        grad_norm,
        enc_all[0],
        dec_all[0],
        down_all[0],
        small_all[0],
        enc_all[1],
        dec_all[1],
        down_all[1],
        small_all[1],
        enc_all[2],
        dec_all[2],
        down_all[2],
        small_all[2],
        shards[3] * factor,
    )


def solution(mesh):
    in_specs = (
        P("dp", "seq", None),
        P("dp", "seq", None),
        P("dp", "seq", None),
        P("dp", "seq"),
        P("dp", "seq"),
        P("dp", "seq"),
        P("dp", "seq"),
        P(("dp", "seq"), None),
        P(("dp", "seq"), None),
        P(("dp", "seq"), None),
        P(("dp", "seq"), None),
        P(("dp", "seq"), None),
        P(("dp", "seq"), None),
        P(("dp", "seq"), None),
        P(("dp", "seq"), None),
        P(("dp", "seq"), None),
        P(("dp", "seq"), None),
        P(("dp", "seq"), None),
        P(("dp", "seq"), None),
    )
    out_specs = (
        P("dp", "seq", None),
        P("dp", "seq", None),
        P("dp", "seq", None),
        P(),
        P(("dp", "seq"), None),
        P(("dp", "seq"), None),
        P(("dp", "seq"), None),
        P(("dp", "seq"), None),
        P(("dp", "seq"), None),
        P(("dp", "seq"), None),
        P(("dp", "seq"), None),
        P(("dp", "seq"), None),
        P(("dp", "seq"), None),
        P(("dp", "seq"), None),
        P(("dp", "seq"), None),
        P(("dp", "seq"), None),
        P(("dp", "seq"), None),
    )
    return jax.shard_map(
        per_device, mesh=mesh, in_specs=in_specs, out_specs=out_specs, check_vma=False
    )
```

profile of v0, /device:TPU:1, one launch (start us, length us, event | category | flops | bytes accessed | tf_op | source)
XLA Modules:
  0.0 2703.5 jit_solution(3392170004736589475)
XLA Ops:
  9.6 180.7 %all-gather = bf16[128,6,31]{2,1,0:T(8,128)(2,1)S(1)} all-gather(bf16[1,6,31]{2,1,0:T(8,128)(2,1)S(1)} %convert_bitcast_fusion.2), channel_id=1, replica_groups=mesh['dp'=32,'seq'=4] {'dp','seq'}, dimensions={0}, use_global_device_ids=true | all-gather | bytes 47988 | tf_op jit(solution)/shard_map/all_gather | solution.py:199
  196.1 26.3 all-gather.20.cloned.1.call-done
  222.3 14.3 reshape.1571
  269.4 23.6 all-gather.10.cloned.1.call-done
  319.6 181.4 %all-gather.14.cloned.1.call-done = bf16[3072,1536]{1,0:T(8,128)(2,1)} async-done(((bf16[24,1536]{1,0:T(8,128)(2,1)}), bf16[3072,1536]{1,0:T(8,128)(2,1)}) %all-gather.14.cloned.1.call-update) | async-done | bytes 9437200 | tf_op jit(solution)/shard_map/all_gather | solution.py:198
  507.2 212.9 %all-gather.18.cloned.1.call-done = bf16[128,6,9216]{2,1,0:T(8,128)(2,1)} async-done(((bf16[1,6,9216]{2,1,0:T(8,128)(2,1)}), bf16[128,6,9216]{2,1,0:T(8,128)(2,1)}) %all-gather.18.cloned.1.call-update) | async-done | bytes 14155792 | tf_op jit(solution)/shard_map/all_gather | solution.py:197
  720.1 18.8 reshape.1569
  817.6 18.1 fusion.83
  889.3 12.0 multiply_reduce_fusion
  995.1 14.4 pad_maximum_fusion.1
  1009.5 18.7 copy.165
  1056.7 544.8 %fusion.1 = f32[8,9216]{1,0:T(8,128)S(1)} fusion(f32[768,9216]{1,0:T(8,128)} %convolution_dynamic-update-slice_fusion), kind=kCustom, calls=%all-reduce-scatter.1 | all-reduce-scatter fusion | flops 9437185 | bytes 28606464
  1606.1 30.4 %collective-permute-start.63 = (f32[6,9216]{1,0:T(8,128)S(1)}, f32[6,9216]{1,0:T(8,128)S(1)}, u32[]{:S(2)}, u32[]{:S(2)}) collective-permute-start(f32[6,9216]{1,0:T(8,128)S(1)} %slice.242), channel_id=1, source_target_pairs={{0,32},{1,33},{2,34},{3,35},{4,36},{5,37},{6,38},{7,39},{8,40},{9,... | collective-permute-start | bytes 663560
  1670.1 26.2 collective-permute-start.39
  1708.8 18.8 collective-permute-start.43
  1741.9 12.3 collective-permute-start.48
  1784.2 18.1 collective-permute-start.54
  1809.8 19.9 collective-permute-start.56
  1856.2 366.8 %fusion = f32[8,6144]{1,0:T(8,128)S(1)} fusion(f32[768,6144]{1,0:T(8,128)} %pad_maximum_fusion), kind=kCustom, calls=%all-reduce-scatter | all-reduce-scatter fusion | flops 6291457 | bytes 19070976
  2299.7 17.9 collective-permute-start.25
  2325.7 138.5 %concatenate.89 = f32[262,9216]{1,0:T(8,128)} concatenate(f32[6,9216]{1,0:T(8,128)} %copy-done.79, f32[8,9216]{1,0:T(8,128)} %collective-permute-done.62, f32[8,9216]{1,0:T(8,128)} %collective-permute-done.61, f32[8,9216]{1,0:T(8,128)} %collective-permute-done.60, f32[8,9216]{1,0:T(8,128)} %collective-permute-done.59, f32[8,9216]{1,0:T(8,128)} %collective-permute-done.58, ...), dimensions={0} | concatenate | bytes 19316736
  2487.2 13.6 collective-permute-done.30
  2508.3 103.2 %concatenate.88 = f32[262,6144]{1,0:T(8,128)} concatenate(f32[6,6144]{1,0:T(8,128)S(1)} %copy-done.112, f32[8,6144]{1,0:T(8,128)} %copy-done.130, f32[8,6144]{1,0:T(8,128)} %copy-done.128, f32[8,6144]{1,0:T(8,128)} %copy-done.127, f32[8,6144]{1,0:T(8,128)} %collective-permute-done.27, f32[8,6144]{1,0:T(8,128)} %collective-permute-done.26, f32[8,6144]{1,0:T(8,128)} %collective-permute-done.25, ...), dimensions={0} | concatenate | bytes 12877824
  2618.2 70.9 %psum.7 = f32[]{:T(128)} all-reduce(f32[]{:T(128)S(6)} %add.468), channel_id=1, replica_groups=mesh['dp'=32,'seq'=4] {'dp','seq'}, use_global_device_ids=true, to_apply=%region_71.72 | all-reduce | flops 1 | bytes 8 | tf_op jit(solution)/shard_map/psum | solution.py:387
  (831 shorter events, 578.4 us)
Async XLA Ops:
  7.2 215.1 %all-gather.20.cloned.1.call-start = ((), (), s32[]{:S(2)}) async-start(), calls=%async_computation.14 | async-start | bytes 12681216 | tf_op jit(solution)/shard_map/all_gather | solution.py:196
  8.8 258.7 %all-gather.12.cloned.1.call-start = ((), (), s32[]{:S(2)}) async-start(), calls=%async_computation.7 | async-start | bytes 1966080 | tf_op jit(solution)/shard_map/all_gather | solution.py:227
  241.6 259.4 %all-gather.14.cloned.1.call-start = ((), (), s32[]{:S(2)}) async-start(), calls=%async_computation.8 | async-start | bytes 9510912 | tf_op jit(solution)/shard_map/all_gather | solution.py:198
  242.3 477.8 %all-gather.18.cloned.1.call-start = ((), (), s32[]{:S(2)}) async-start(), calls=%async_computation.13 | async-start | bytes 19021824 | tf_op jit(solution)/shard_map/all_gather | solution.py:197
  243.1 525.4 %all-gather.16.cloned.1.call-start = ((), (), s32[]{:S(2)}) async-start(), calls=%async_computation.9 | async-start | bytes 1966080 | tf_op jit(solution)/shard_map/all_gather | solution.py:253
  507.1 366.0 %reduce-scatter.18.cloned.1.call-start = ((), (), s32[]{:S(2)}) async-start(), calls=%async_computation.10 | async-start | bytes 1966080 | tf_op jit(solution)/shard_map/reduce_scatter | solution.py:271
  835.7 111.7 %reduce-scatter.24.cloned.1.call-start = ((), (), s32[]{:S(2)}) async-start(), calls=%async_computation.15 | async-start | bytes 983040
  861.4 88.1 %reduce-scatter.26.cloned.1.call-start = ((), (), s32[]{:S(2)}) async-start(), calls=%async_computation.16 | async-start | bytes 983040
  873.1 110.7 %reduce-scatter.20.cloned.1.call-start = ((), (), s32[]{:S(2)}) async-start(), calls=%async_computation.11 | async-start | bytes 1966080 | tf_op jit(solution)/shard_map/reduce_scatter | solution.py:335
  912.6 71.2 %reduce-scatter.22.cloned.1.call-start = ((), (), s32[]{:S(2)}) async-start(), calls=%async_computation.12 | async-start | bytes 1966080 | tf_op jit(solution)/shard_map/reduce_scatter | solution.py:338
  922.3 1584.5 %all-reduce.8.cloned.1.call-start = ((), (), s32[]{:S(2)}) async-start(), calls=%async_computation.18 | async-start | bytes 196608
  994.9 1619.9 %reduce-scatter.28.cloned.1.call-start = ((), (), s32[]{:S(2)}) async-start(), calls=%async_computation.17 | async-start | bytes 19021824 | tf_op jit(solution)/shard_map/reduce_scatter | solution.py:368
  1601.5 64.4 %collective-permute-start.32 = (f32[8,9216]{1,0:T(8,128)S(1)}, f32[8,9216]{1,0:T(8,128)S(1)}, u32[]{:S(2)}, u32[]{:S(2)}) collective-permute-start(f32[8,9216]{1,0:T(8,128)S(1)} %fusion.1), channel_id=1, source_target_pairs={{0,1},{1,2},{2,3},{3,4},{4,5},{5,6},{6,7},{7,8},{8,9},{9,10},{10,1... | collective-permute-start | bytes 884744
  1784.2 63.2 %collective-permute-start.54 = (f32[8,9216]{1,0:T(8,128)S(1)}, f32[8,9216]{1,0:T(8,128)S(1)}, u32[]{:S(2)}, u32[]{:S(2)}) collective-permute-start(f32[8,9216]{1,0:T(8,128)S(1)} %fusion.1), channel_id=1, source_target_pairs={{0,23},{1,24},{2,25},{3,26},{4,27},{5,28},{6,29},{7,30},{8,31},{9,... | collective-permute-start | bytes 884744
  1838.7 384.4 %collective-permute-start.58 = (f32[8,9216]{1,0:T(8,128)S(1)}, f32[8,9216]{1,0:T(8,128)}, u32[]{:S(2)}, u32[]{:S(2)}) collective-permute-start(f32[8,9216]{1,0:T(8,128)S(1)} %fusion.1), channel_id=1, source_target_pairs={{0,27},{1,28},{2,29},{3,30},{4,31},{5,32},{6,33},{7,34},{8,35},{9,... | collective-permute-start | bytes 884744
  1847.4 377.7 %collective-permute-start.59 = (f32[8,9216]{1,0:T(8,128)S(1)}, f32[8,9216]{1,0:T(8,128)}, u32[]{:S(2)}, u32[]{:S(2)}) collective-permute-start(f32[8,9216]{1,0:T(8,128)S(1)} %fusion.1), channel_id=1, source_target_pairs={{0,28},{1,29},{2,30},{3,31},{4,32},{5,33},{6,34},{7,35},{8,36},{9,... | collective-permute-start | bytes 884744
  1849.4 377.0 %collective-permute-start.60 = (f32[8,9216]{1,0:T(8,128)S(1)}, f32[8,9216]{1,0:T(8,128)}, u32[]{:S(2)}, u32[]{:S(2)}) collective-permute-start(f32[8,9216]{1,0:T(8,128)S(1)} %fusion.1), channel_id=1, source_target_pairs={{0,29},{1,30},{2,31},{3,32},{4,33},{5,34},{6,35},{7,36},{8,37},{9,... | collective-permute-start | bytes 884744
  1851.4 377.0 %collective-permute-start.61 = (f32[8,9216]{1,0:T(8,128)S(1)}, f32[8,9216]{1,0:T(8,128)}, u32[]{:S(2)}, u32[]{:S(2)}) collective-permute-start(f32[8,9216]{1,0:T(8,128)S(1)} %fusion.1), channel_id=1, source_target_pairs={{0,30},{1,31},{2,32},{3,33},{4,34},{5,35},{6,36},{7,37},{8,38},{9,... | collective-permute-start | bytes 884744
  1854.2 376.2 %collective-permute-start.62 = (f32[8,9216]{1,0:T(8,128)S(1)}, f32[8,9216]{1,0:T(8,128)}, u32[]{:S(2)}, u32[]{:S(2)}) collective-permute-start(f32[8,9216]{1,0:T(8,128)S(1)} %fusion.1), channel_id=1, source_target_pairs={{0,31},{1,32},{2,33},{3,34},{4,35},{5,36},{6,37},{7,38},{8,39},{9,... | collective-permute-start | bytes 884744
  2295.6 170.6 %collective-permute-start.23 = (f32[8,6144]{1,0:T(8,128)S(1)}, f32[8,6144]{1,0:T(8,128)}, u32[]{:S(2)}, u32[]{:S(2)}) collective-permute-start(f32[8,6144]{1,0:T(8,128)S(1)} %fusion), channel_id=1, source_target_pairs={{0,24},{1,25},{2,26},{3,27},{4,28},{5,29},{6,30},{7,31},{8,32},{9,... | collective-permute-start | bytes 589832
  2297.5 169.9 %collective-permute-start.24 = (f32[8,6144]{1,0:T(8,128)S(1)}, f32[8,6144]{1,0:T(8,128)}, u32[]{:S(2)}, u32[]{:S(2)}) collective-permute-start(f32[8,6144]{1,0:T(8,128)S(1)} %fusion), channel_id=1, source_target_pairs={{0,25},{1,26},{2,27},{3,28},{4,29},{5,30},{6,31},{7,32},{8,33},{9,... | collective-permute-start | bytes 589832
  2299.7 169.0 %collective-permute-start.25 = (f32[8,6144]{1,0:T(8,128)S(1)}, f32[8,6144]{1,0:T(8,128)}, u32[]{:S(2)}, u32[]{:S(2)}) collective-permute-start(f32[8,6144]{1,0:T(8,128)S(1)} %fusion), channel_id=1, source_target_pairs={{0,26},{1,27},{2,28},{3,29},{4,30},{5,31},{6,32},{7,33},{8,34},{9,... | collective-permute-start | bytes 589832
  2317.6 152.4 %collective-permute-start.26 = (f32[8,6144]{1,0:T(8,128)S(1)}, f32[8,6144]{1,0:T(8,128)}, u32[]{:S(2)}, u32[]{:S(2)}) collective-permute-start(f32[8,6144]{1,0:T(8,128)S(1)} %fusion), channel_id=1, source_target_pairs={{0,27},{1,28},{2,29},{3,30},{4,31},{5,32},{6,33},{7,34},{8,35},{9,... | collective-permute-start | bytes 589832
  2322.7 148.7 %collective-permute-start.27 = (f32[8,6144]{1,0:T(8,128)S(1)}, f32[8,6144]{1,0:T(8,128)}, u32[]{:S(2)}, u32[]{:S(2)}) collective-permute-start(f32[8,6144]{1,0:T(8,128)S(1)} %fusion), channel_id=1, source_target_pairs={{0,28},{1,29},{2,30},{3,31},{4,32},{5,33},{6,34},{7,35},{8,36},{9,... | collective-permute-start | bytes 589832
  (288 other events, 13633.6 us)
Sparse Core Ops, SparseCore 0:
  10.3 211.9 all-gather.19
  241.0 23.9 all-gather.11
  267.3 25.6 all-gather.9
  295.1 205.8 all-gather.13
  503.1 216.9 all-gather.17
  722.2 24.7 all-gather.15
  835.8 24.6 reduce-scatter.17
  863.0 20.3 reduce-scatter.23
  885.8 19.9 reduce-scatter.25
  912.7 24.6 reduce-scatter.19
  939.8 24.8 reduce-scatter.21
  995.0 139.7 all-reduce.7
  1137.3 679.2 reduce-scatter.27
where the time goes:
time: 2720 us; the launch traced here: 2700 us
  blocking collectives  1200 us (44%)
  waiting for transfers between devices  460 us (17%)
  local copies, waits for them, and re-layouts  383 us (14%)
  starting transfers between devices  361 us (13%)
  matrix products  198 us (7%)
  other arithmetic  76.7 us (3%)
    unnamed x2, blocking collectives  912 us
    unnamed x67, starting transfers between devices  360 us
    unnamed x486, local copies, waits for them, and re-layouts  332 us
    all_gather x1, waiting for transfers between devices, per_device(): lax.all_gather(dec_master.astype(jnp.bfloat16), ('dp', 'seq'), axis=0, ti...  213 us
    all_gather x1, waiting for transfers between devices, per_device(): lax.all_gather(down_master.astype(jnp.bfloat16), ('dp', 'seq'), axis=0, t...  181 us
    all_gather x1, blocking collectives, per_device(): lax.all_gather(small_master.astype(jnp.bfloat16), ('dp', 'seq'), axis=0,...  181 us
    psum x1, blocking collectives, per_device(): grad_norm = jnp.sqrt(lax.psum(squares, ('dp', 'seq')))  70.9 us
  transfers between devices with their start and end apart: 77, of which 6 were waited for; matrix products, arithmetic and copies ran while one was open for 54% of the time, Pallas kernels for 0%

commit v1 on v0

v1 whole, which is shorter than its diff:
```python
import jax
import jax.numpy as jnp
import numpy as np
from jax import lax
from jax.experimental import pallas as pl
from jax.experimental.pallas import tpu as pltpu
from jax.sharding import Mesh, PartitionSpec as P

HEAD = 64
STEP = 10
NORM_EPS = 1e-05
MASKED = -1000000000.0
BETA_FIRST = 0.9
BETA_SECOND = 0.999
ADAM_EPS = 1e-08
RATE_MATRIX = 0.1
RATE_SMALL = 0.5
DECAY_RATE = 0.01
CLIP_LEVEL = 1.0
BF = jnp.bfloat16
F32 = jnp.float32
PAIR = 2 * HEAD
LANES = 128
ROW_AXES = ("z", "xh", "y")
POS_AXES = ("xl", "c")
ALL_AXES = ("z", "xh", "y", "xl", "c")
SWAP = [(0, 1), (1, 0)]


def swap(value, axis):
    return lax.ppermute(value, axis, SWAP)


def join_core(value):
    return jnp.concatenate([value, swap(value, "c")], axis=0)


def sum_core(partial):
    mine = partial.shape[0] // 2
    return partial[:mine] + swap(partial[mine:], "c")


def swap_z(value):
    other = lax.ppermute(value, ("z", "c"), [(1, 4), (4, 1), (3, 6), (6, 3)])
    moved = (lax.axis_index("z") // 2) != lax.axis_index("c")
    return jnp.where(moved, other, value)


def feature_order(width):
    rest = width // 32
    new = np.arange(width)
    z, y, xh, r = new // (8 * rest), (new // (2 * rest)) % 4, (new // rest) % 2, new % rest
    old = ((z * 2 + xh) * 4 + y) * rest + r
    return old


def head_order(width):
    r = width // 128
    own = np.arange(width // 2)
    z, xh, y, xl, c, i = (
        own // (32 * r) // 2,
        (own // (16 * r)) % 2,
        (own // (4 * r)) % 4,
        (own // (2 * r)) % 2,
        (own // r) % 2,
        own % r,
    )
    z = own // (32 * r)
    places = []
    for half in range(2):
        place = (((((c * 2 + z) * 4 + y) * 2 + xh) * 2 + xl) * 2 + half) * r + i
        places.append(place)
    return np.concatenate(places)


def one_hot(picks, width):
    rows = lax.broadcasted_iota(jnp.int32, (width, len(picks)), 0)
    return (rows == jnp.asarray(picks, jnp.int32)[None, :]).astype(BF)


def dot(left, right, kind=F32):
    return jnp.dot(left, right, preferred_element_type=kind)


def dot_t(left, right, kind=F32):
    return lax.dot_general(left, right, (((0,), (0,)), ((), ())), preferred_element_type=kind)


def dot_b(left, right, kind=F32):
    return lax.dot_general(left, right, (((1,), (1,)), ((), ())), preferred_element_type=kind)


def two_parts(value):
    high = lax.reduce_precision(value, 8, 7)
    return high.astype(BF), (value - high).astype(BF)


def reorder_wide(value, order):
    high, low = two_parts(value)
    both = dot_b(jnp.concatenate([high, low], axis=0), order)
    return both[: value.shape[0]] + both[value.shape[0] :]


def norm_stats(x):
    center = x - jnp.mean(x, axis=-1, keepdims=True)
    spread = jnp.mean(center * center, axis=-1, keepdims=True)
    scale = lax.rsqrt(spread + NORM_EPS)
    return center * scale, scale


def norm(x, gain, shift):
    unit, scale = norm_stats(x)
    return (unit * gain + shift).astype(BF)


def norm_back(x, gain, gradient):
    unit, scale = norm_stats(x)
    inner = gradient * gain
    back = scale * (
        inner
        - jnp.mean(inner, axis=-1, keepdims=True)
        - unit * jnp.mean(inner * unit, axis=-1, keepdims=True)
    )
    return back, jnp.sum(gradient * unit, axis=0), jnp.sum(gradient, axis=0)


def gelu_parts(u):
    cdf = 0.5 * (1.0 + lax.erf(u * (0.5**0.5)))
    pdf = jnp.exp(-0.5 * u * u) * (1.0 / np.sqrt(2.0 * np.pi)).astype(np.float32)
    return u * cdf, cdf + u * pdf


def lane_mask(value, which):
    lane = lax.broadcasted_iota(jnp.int32, value.shape, 1)
    return jnp.where((lane // HEAD) == which, value, jnp.zeros_like(value))


def allowed_of(causal, ids_ref, qid_ref, part):
    seg = ids_ref[part, :, 0:1] == qid_ref[0:1, :]
    if causal:
        seg = seg & (ids_ref[part, :, 1:2] <= qid_ref[1:2, :])
    return seg


def scores_t(keys, query, allowed):
    raw = lax.dot_general(keys, query, (((1,), (1,)), ((), ())), preferred_element_type=F32)
    return jnp.where(allowed, raw, MASKED)


def attend_kernel(causal, q_ref, k0_ref, v0_ref, k1_ref, v1_ref, ids_ref, qid_ref, o_ref, lse_ref):
    query = q_ref[...] * jnp.asarray(HEAD**-0.5, BF)
    allowed = [allowed_of(causal, ids_ref, qid_ref, part) for part in range(2)]
    mixed = []
    for head in range(2):
        one = lane_mask(query, head)
        scores = [scores_t(ref[...], one, ok) for ref, ok in zip((k0_ref, k1_ref), allowed)]
        top = jnp.maximum(
            jnp.max(scores[0], axis=0, keepdims=True), jnp.max(scores[1], axis=0, keepdims=True)
        )
        expo = [jnp.exp(s - top) for s in scores]
        total = jnp.sum(expo[0], axis=0, keepdims=True) + jnp.sum(expo[1], axis=0, keepdims=True)
        share = 1.0 / total
        out = 0.0
        for ref, e in zip((v0_ref, v1_ref), expo):
            out = out + lax.dot_general(
                ref[...], (e * share).astype(BF), (((0,), (0,)), ((), ())), preferred_element_type=F32
            )
        mixed.append(out)
        lse_ref[0, head : head + 1, :] = top + jnp.log(total)
    both = jnp.concatenate([mixed[0][:HEAD], mixed[1][HEAD:]], axis=0)
    o_ref[...] = both.T.astype(BF)


def attend_back_kernel(
    causal, q_ref, k0_ref, v0_ref, k1_ref, v1_ref, g_ref, ids_ref, qid_ref, lse_ref,
    dq_ref, dk0_ref, dv0_ref, dk1_ref, dv1_ref,
):
    query = q_ref[...] * jnp.asarray(HEAD**-0.5, BF)
    grad = g_ref[...]
    allowed = [allowed_of(causal, ids_ref, qid_ref, part) for part in range(2)]
    keys = (k0_ref[...], k1_ref[...])
    values = (v0_ref[...], v1_ref[...])
    grad_q = 0.0
    grad_k = [0.0, 0.0]
    grad_v = [0.0, 0.0]
    for head in range(2):
        one = lane_mask(query, head)
        grad_one = lane_mask(grad, head)
        lse = lse_ref[0, head : head + 1, :]
        probs = [jnp.exp(scores_t(k, one, ok) - lse) for k, ok in zip(keys, allowed)]
        grad_p = [
            lax.dot_general(v, grad_one, (((1,), (1,)), ((), ())), preferred_element_type=F32)
            for v in values
        ]
        inner = jnp.sum(probs[0] * grad_p[0], axis=0, keepdims=True) + jnp.sum(
            probs[1] * grad_p[1], axis=0, keepdims=True
        )
        for part in range(2):
            grad_s = (probs[part] * (grad_p[part] - inner)).astype(BF)
            grad_v[part] = grad_v[part] + dot(probs[part].astype(BF), grad_one)
            grad_k[part] = grad_k[part] + dot(grad_s, one)
            grad_q = grad_q + lax.dot_general(
                lane_mask(keys[part], head), grad_s, (((0,), (0,)), ((), ())),
                preferred_element_type=F32,
            )
    dq_ref[...] = (grad_q * HEAD**-0.5).T.astype(BF)
    dk0_ref[...] = grad_k[0]
    dv0_ref[...] = grad_v[0]
    dk1_ref[...] = grad_k[1].astype(BF)
    dv1_ref[...] = grad_v[1].astype(BF)


def call_kernel(body, causal, arrays, ids, qid, extra, out_shape, out_specs, cost):
    in_specs = [
        pl.BlockSpec((a.shape[0], PAIR), lambda p, at=at: (0, at + p)) for a, at in arrays
    ]
    in_specs.append(pl.BlockSpec(ids.shape, lambda p: (0, 0, 0)))
    in_specs.append(pl.BlockSpec(qid.shape, lambda p: (0, 0)))
    in_specs += [pl.BlockSpec((1,) + e.shape[1:], lambda p: (p, 0, 0)) for e in extra]

    def kernel(*refs):
        body(causal, *refs)

    pairs = extra[0].shape[0] if extra else out_shape[1].shape[0]
    return pl.pallas_call(
        kernel,
        grid=(pairs,),
        in_specs=in_specs,
        out_specs=out_specs,
        out_shape=out_shape,
        compiler_params=pltpu.CompilerParams(vmem_limit_bytes=56 * 1024 * 1024),
        cost_estimate=cost,
    )(*[a for a, at in arrays], ids, qid, *extra)


def cost_of(n_q, n_k, width, products):
    return pl.CostEstimate(
        flops=4 * 2 * products * n_q * n_k * width,
        bytes_accessed=4 * (n_q + n_k) * width,
        transcendentals=n_q * n_k * width // HEAD,
    )


def attend_fwd(causal, arrays, ids, qid, pairs):
    n_q = qid.shape[1]
    out_shape = (
        jax.ShapeDtypeStruct((n_q, pairs * PAIR), BF),
        jax.ShapeDtypeStruct((pairs, 2, n_q), F32),
    )
    out_specs = (
        pl.BlockSpec((n_q, PAIR), lambda p: (0, p)),
        pl.BlockSpec((1, 2, n_q), lambda p: (p, 0, 0)),
    )
    return call_kernel(
        attend_kernel, causal, arrays, ids, qid, (), out_shape, out_specs,
        cost_of(n_q, 2 * ids.shape[1], pairs * PAIR, 2),
    )


def attend_back(causal, arrays, grad, ids, qid, lse):
    pairs, n_q, n_k = lse.shape[0], qid.shape[1], ids.shape[1]
    wide = pairs * PAIR
    out_shape = (
        jax.ShapeDtypeStruct((n_q, wide), BF),
        jax.ShapeDtypeStruct((n_k, wide), F32),
        jax.ShapeDtypeStruct((n_k, wide), F32),
        jax.ShapeDtypeStruct((n_k, wide), BF),
        jax.ShapeDtypeStruct((n_k, wide), BF),
    )
    out_specs = tuple(pl.BlockSpec((s.shape[0], PAIR), lambda p: (0, p)) for s in out_shape)
    return call_kernel(
        attend_back_kernel, causal, list(arrays) + [(grad, 0)], ids, qid, (lse,), out_shape, out_specs,
        cost_of(n_q, 2 * n_k, wide, 5),
    )


def adam_step(master, first, second, gradient, factor, rate, decay):
    clipped = gradient * factor
    first_new = BETA_FIRST * first + (1 - BETA_FIRST) * clipped
    second_new = BETA_SECOND * second + (1 - BETA_SECOND) * clipped * clipped
    first_hat = first_new / (1 - BETA_FIRST**STEP)
    second_hat = second_new / (1 - BETA_SECOND**STEP)
    master_new = master - rate * (first_hat / (jnp.sqrt(second_hat) + ADAM_EPS) + decay * master)
    return (master_new, first_new, second_new)


def per_device(
    src_x, tgt_x, out_cot, src_seg, tgt_seg, src_pad, tgt_pad,
    enc_master, dec_master, down_master, small_master,
    enc_first, dec_first, down_first, small_first,
    enc_second, dec_second, down_second, small_second,
):
    width = src_x.shape[-1]
    half = width // 2
    hid = 2 * width
    pairs = half // PAIR
    rows = enc_master.shape[0]
    down_rows = down_master.shape[0]
    n_small = small_master.shape[1]
    core = lax.axis_index("c")
    first_core = core == 0
    order = one_hot(feature_order(width), width)
    place = one_hot(head_order(width), width)

    encb, decb, downb = enc_master.astype(BF), dec_master.astype(BF), down_master.astype(BF)
    smallb = jnp.pad(small_master.astype(BF), ((0, 0), (0, LANES - n_small)))

    def block(matrix, index):
        return matrix[:, index * width : (index + 1) * width]

    def halves(matrix):
        n = matrix.shape[1] // 2
        return matrix[:, :n], matrix[:, n:]

    col_blocks = [
        halves(block(encb, 0)), halves(block(encb, 1)), halves(block(encb, 2)), (smallb, smallb),
        halves(encb[:, 4 * width :]),
        halves(block(decb, 0)), halves(block(decb, 1)), halves(block(decb, 2)),
        halves(block(decb, 4)), halves(block(decb, 5)), halves(block(decb, 6)),
        halves(decb[:, 8 * width :]),
    ]
    cols0 = jnp.concatenate([b[0] for b in col_blocks], axis=1)
    cols1 = jnp.concatenate([b[1] for b in col_blocks], axis=1)
    mine = jnp.where(first_core, cols0, cols1)
    theirs = swap(jnp.where(first_core, cols1, cols0), "c")
    cols = jnp.concatenate(
        [jnp.where(first_core, mine, theirs), jnp.where(first_core, theirs, mine)], axis=0
    )
    cols = lax.all_gather(cols, ("xh", "xl"), axis=0, tiled=True)

    row_shard = jnp.concatenate(
        [block(encb, 3), block(decb, 3), block(decb, 7), downb[:, :width], downb[:, width:]], axis=0
    )
    row_shard = swap_z(dot(row_shard, order, BF))
    row_shard = lax.all_gather(row_shard, ("xh", "xl"), axis=0)

    def pack_out(index):
        part = row_shard[:, index * rows : (index + 1) * rows].reshape(4, rows, 2, half)
        return part.transpose(0, 2, 1, 3).reshape(8 * rows, half)

    def pack_down(index):
        at = 3 * rows + index * down_rows
        part = row_shard[:, at : at + down_rows].reshape(2, 2 * down_rows, width)
        return [part[0], part[1]]

    n_qkv, n_one = 3 * half, 3 * half + LANES
    n_two, n_three = n_one + hid, n_one + hid + 6 * half
    shard_one = cols[:, :n_one]
    shard_two = jnp.concatenate([pack_out(0), cols[:, n_one:n_two]] + pack_down(0), axis=1)
    shard_three = jnp.concatenate([cols[:, n_two:n_three], pack_out(1), pack_out(2)], axis=1)
    shard_four = jnp.concatenate([cols[:, n_three:]] + pack_down(1), axis=1)

    def spread(shard):
        return lax.all_gather(shard, ("z", "y"), axis=0, tiled=True)

    full_one, full_two, full_three, full_four = (
        spread(shard_one), spread(shard_two), spread(shard_three), spread(shard_four),
    )

    def unpack_out(part):
        natural = dot_t(place, part, BF)
        return jnp.concatenate([natural[:half], natural[half:]], axis=1)

    def repack_out(grad):
        stacked = jnp.concatenate([grad[:, :half], grad[:, half:]], axis=0)
        return dot(place, stacked, BF)

    def unpack_down(part):
        part = jnp.stack([part[:, :width], part[:, width:]], axis=0)
        part = part.reshape(2, 2, 2, 4, 2, down_rows, width)
        return part.transpose(2, 0, 3, 4, 1, 5, 6).reshape(hid, width)

    def repack_down(grad):
        part = grad.reshape(2, 2, 4, 2, 2, down_rows, width)
        part = part.transpose(1, 4, 0, 2, 3, 5, 6).reshape(2, width, width)
        return [part[0], part[1]]

    w_eqkv, small_all = full_one[:, :n_qkv], full_one[:, n_qkv:]
    w_eo = unpack_out(full_two[:, :half])
    w_e1 = full_two[:, half : half + hid]
    w_e2 = unpack_down(full_two[:, half + hid :])
    w_dqkv = full_three[:, :n_qkv]
    w_cq = full_three[:, n_qkv : 4 * half]
    w_ckv = full_three[:, 4 * half : 6 * half]
    w_so = unpack_out(full_three[:, 6 * half : 7 * half])
    w_co = unpack_out(full_three[:, 7 * half :])
    w_d1 = full_four[:, :hid]
    w_d2 = unpack_down(full_four[:, hid:])

    eye = one_hot(np.arange(width), width)
    small_p = dot_t(small_all, eye)
    small_own = dot_b(small_all.T, order)

    def own_half(column):
        row = small_own[column]
        return jnp.where(first_core, row[:half], row[half:])

    def hidden_bias(column):
        low = jnp.concatenate([small_own[column], small_own[column + 1]])
        high = jnp.concatenate([small_own[column + 2], small_own[column + 3]])
        return jnp.where(first_core, low, high)

    none = jnp.zeros((half,), F32)

    def ids_of(seg, pad, at):
        n = seg.shape[1]
        spot = (lax.axis_index("xl") * 2 + core) * n + jnp.arange(n, dtype=jnp.int32)
        key = jnp.where(pad[0] == 1, seg[0], -1)
        return jnp.stack([key, spot, seg[0]], axis=1)

    src_ids = join_core(ids_of(src_seg, src_pad, 0))
    tgt_ids = join_core(ids_of(tgt_seg, tgt_pad, 0))
    src_keys = jnp.stack([src_ids[:, :2], swap(src_ids[:, :2], "xl")])
    tgt_keys = jnp.stack([tgt_ids[:, :2], swap(tgt_ids[:, :2], "xl")])
    src_q = jnp.stack([src_ids[:, 2], src_ids[:, 1]])
    tgt_q = jnp.stack([tgt_ids[:, 2], tgt_ids[:, 1]])

    source = dot(src_x[0], order)
    enc_norm = join_core(norm(source, small_p[0], small_p[1]))
    enc_qkv = (dot(enc_norm, w_eqkv) + jnp.concatenate([own_half(2), none, own_half(3)])).astype(BF)
    enc_far = swap(enc_qkv[:, half:], "xl")
    enc_arrays = [(enc_qkv, 0), (enc_qkv, pairs), (enc_qkv, 2 * pairs), (enc_far, 0), (enc_far, pairs)]

    target = dot(tgt_x[0], order)
    dec_norm = join_core(norm(target, small_p[14], small_p[15]))

    enc_att, enc_lse = attend_fwd(False, enc_arrays, src_keys, src_q, pairs)
    enc_one = source + sum_core(dot(enc_att, w_eo)) + small_p[4]

    def feed_fwd(resid, w_in, w_out, base):
        normed = join_core(norm(resid, small_p[base], small_p[base + 1]))
        active, slope = gelu_parts(dot(normed, w_in) + hidden_bias(base + 3))
        active = active.astype(BF)
        return normed, active, slope, resid + sum_core(dot(active, w_out)) + small_p[base + 2]

    enc_ffn = feed_fwd(enc_one, w_e1, w_e2, 5)
    enc_two = enc_ffn[3]
    memory = join_core(norm(enc_two, small_p[12], small_p[13]))

    dec_qkv = (dot(dec_norm, w_dqkv) + jnp.concatenate([own_half(16), none, own_half(17)])).astype(BF)
    dec_far = swap(dec_qkv[:, half:], "xl")
    dec_arrays = [(dec_qkv, 0), (dec_qkv, pairs), (dec_qkv, 2 * pairs), (dec_far, 0), (dec_far, pairs)]
    self_att, self_lse = attend_fwd(True, dec_arrays, tgt_keys, tgt_q, pairs)
    dec_one = target + sum_core(dot(self_att, w_so)) + small_p[18]
    cross_norm = join_core(norm(dec_one, small_p[19], small_p[20]))
    cross_q = (dot(cross_norm, w_cq) + own_half(21)).astype(BF)
    cross_kv = (dot(memory, w_ckv) + jnp.concatenate([none, own_half(22)])).astype(BF)
    cross_far = swap(cross_kv, "xl")
    cross_arrays = [(cross_q, 0), (cross_kv, 0), (cross_kv, pairs), (cross_far, 0), (cross_far, pairs)]
    cross_att, cross_lse = attend_fwd(False, cross_arrays, src_keys, tgt_q, pairs)
    dec_two = dec_one + sum_core(dot(cross_att, w_co)) + small_p[23]
    dec_ffn = feed_fwd(dec_two, w_d1, w_d2, 24)
    dec_out = reorder_wide(dec_ffn[3], order)

    small_grad = {}
    own_grad = {}

    def put_own(column, row):
        empty = jnp.zeros_like(row)
        own_grad[column] = jnp.where(
            first_core, jnp.concatenate([row, empty]), jnp.concatenate([empty, row])
        )

    def put_hidden(column, row):
        empty = jnp.zeros_like(row)
        low, high = jnp.where(first_core, row, empty), jnp.where(first_core, empty, row)
        for j, part in enumerate((low[:width], low[width:], high[:width], high[width:])):
            own_grad[column + j] = part

    def feed_back(resid, saved, w_in, w_out, base, gradient):
        normed, active, slope = saved[:3]
        branch = gradient.astype(BF)
        small_grad[base + 2] = jnp.sum(branch, axis=0, dtype=F32)
        branch = join_core(branch)
        grad_out = dot_t(active, branch, BF)
        grad_hidden = (dot_b(branch, w_out) * slope).astype(BF)
        put_hidden(base + 3, jnp.sum(grad_hidden, axis=0, dtype=F32))
        grad_in = dot_t(normed, grad_hidden, BF)
        grad_normed = sum_core(dot_b(grad_hidden, w_in))
        back, small_grad[base], small_grad[base + 1] = norm_back(resid, small_p[base], grad_normed)
        return gradient + back, grad_in, grad_out

    def out_back(gradient, attended, weight, column):
        branch = gradient.astype(BF)
        small_grad[column] = jnp.sum(branch, axis=0, dtype=F32)
        branch = join_core(branch)
        return dot_t(attended, branch, BF), dot_b(branch, weight, BF)

    def in_back(resid, normed, grad_proj, weight, column, gradient):
        grad_normed = sum_core(dot_b(grad_proj, weight))
        back, small_grad[column], small_grad[column + 1] = norm_back(
            resid, small_p[column], grad_normed
        )
        return gradient + back, dot_t(normed, grad_proj, BF)

    def gather_back(near_k, near_v, far_k, far_v):
        far = swap(jnp.concatenate([far_k, far_v], axis=1), "xl")
        return (jnp.concatenate([near_k, near_v], axis=1) + far).astype(BF)

    def reduce(parts):
        return lax.psum_scatter(
            jnp.concatenate(parts, axis=1), ("z", "y"), scatter_dimension=0, tiled=True
        )

    top = dot(out_cot[0], order)
    grad_two, g_d1, g_d2 = feed_back(dec_two, dec_ffn, w_d1, w_d2, 24, top)
    sum_four = reduce([g_d1] + repack_down(g_d2))

    g_co, grad_att = out_back(grad_two, cross_att, w_co, 23)
    cross_gq, ck0, cv0, ck1, cv1 = attend_back(
        False, cross_arrays, grad_att, src_keys, tgt_q, cross_lse
    )
    cross_gkv = gather_back(ck0, cv0, ck1, cv1)
    put_own(21, jnp.sum(cross_gq, axis=0, dtype=F32))
    put_own(22, jnp.sum(cross_gkv[:, half:], axis=0, dtype=F32))
    grad_one, g_cq = in_back(dec_one, cross_norm, cross_gq, w_cq, 19, grad_two)

    g_so, grad_att = out_back(grad_one, self_att, w_so, 18)
    self_gq, sk0, sv0, sk1, sv1 = attend_back(True, dec_arrays, grad_att, tgt_keys, tgt_q, self_lse)
    self_grad = jnp.concatenate([self_gq, gather_back(sk0, sv0, sk1, sv1)], axis=1)
    self_sum = jnp.sum(self_grad, axis=0, dtype=F32)
    put_own(16, self_sum[:half])
    put_own(17, self_sum[2 * half :])
    tgt_grad, g_dqkv = in_back(target, dec_norm, self_grad, w_dqkv, 14, grad_one)
    tgt_grad = reorder_wide(tgt_grad, order)

    g_ckv = dot_t(memory, cross_gkv, BF)
    sum_three = reduce([g_dqkv, g_cq, g_ckv, repack_out(g_so), repack_out(g_co)])
    grad_memory = sum_core(dot_b(cross_gkv, w_ckv))
    grad_memory = lax.reduce_precision(grad_memory, 8, 7)
    enc_grad_two, small_grad[12], small_grad[13] = norm_back(enc_two, small_p[12], grad_memory)

    enc_grad_one, g_e1, g_e2 = feed_back(enc_one, enc_ffn, w_e1, w_e2, 5, enc_grad_two)
    g_eo, grad_att = out_back(enc_grad_one, enc_att, w_eo, 4)
    spare = jnp.zeros((width, LANES), BF)
    sum_two = reduce([repack_out(g_eo), g_e1] + repack_down(g_e2) + [spare])
    enc_gq, ek0, ev0, ek1, ev1 = attend_back(False, enc_arrays, grad_att, src_keys, src_q, enc_lse)
    enc_grad = jnp.concatenate([enc_gq, gather_back(ek0, ev0, ek1, ev1)], axis=1)
    enc_sum = jnp.sum(enc_grad, axis=0, dtype=F32)
    put_own(2, enc_sum[:half])
    put_own(3, enc_sum[2 * half :])
    src_grad, g_eqkv = in_back(source, enc_norm, enc_grad, w_eqkv, 0, enc_grad_one)
    src_grad = reorder_wide(src_grad, order)

    empty = jnp.zeros((width,), F32)
    stored = jnp.stack([small_grad.get(j, empty) for j in range(LANES)]).astype(BF)
    owned = jnp.stack([own_grad.get(j, empty) for j in range(LANES)]).astype(BF)
    g_small = (dot_b(eye, stored) + lax.dot_general(
        order, owned, (((0,), (1,)), ((), ())), preferred_element_type=F32
    )).astype(BF)
    sum_one = reduce([g_eqkv, g_small])

    xh, xl = lax.axis_index("xh"), lax.axis_index("xl")

    def pick(which, low, high):
        return jnp.where(which == 0, low, high), jnp.where(which == 0, high, low)

    def sum_x(value):
        n = value.shape[0] // 2
        keep, send = pick(xh, value[:n], value[n:])
        value = keep.astype(F32) + swap(send, "xh").astype(F32)
        n = n // 2
        keep, send = pick(xl, value[:n], value[n:])
        return keep + swap(send.astype(BF), "xl").astype(F32)

    def sum_x_down(value):
        keep, send = pick(xh, value[:, :width], value[:, width:])
        value = keep.astype(F32) + swap(send, "xh").astype(F32)
        keep, send = pick(xl, value[:down_rows], value[down_rows:])
        return keep + swap(send.astype(BF), "xl").astype(F32)

    def from_cores(value):
        keep, send = pick(core, value[:rows], value[rows:])
        other = swap(send, "c")
        return pick(core, keep, other)

    def wide(low, high, start, stop):
        return [jnp.concatenate([low[:, start:stop], high[:, start:stop]], axis=1)]

    def own_columns(shards):
        shards = swap_z(jnp.concatenate(shards, axis=0))
        return reorder_wide(shards, order)

    def out_shard(value):
        return jnp.concatenate([value[:rows], value[rows:]], axis=1)

    cols = sum_x(jnp.concatenate(
        [sum_one, sum_two[:, : half + hid], sum_three, sum_four[:, :hid]], axis=1
    ))
    at_two = n_one + half
    at_three = at_two + hid
    at_four = at_three + 8 * half
    low, high = from_cores(jnp.concatenate(
        [cols[:, :n_one], cols[:, at_two : at_three + 6 * half], cols[:, at_four:]], axis=1
    ))
    outs = own_columns([
        out_shard(cols[:, n_one:at_two]),
        out_shard(cols[:, at_three + 6 * half : at_three + 7 * half]),
        out_shard(cols[:, at_three + 7 * half : at_four]),
        sum_x_down(sum_two[:, half + hid : half + hid + 2 * width]),
        sum_x_down(sum_four[:, hid:]),
    ])

    def pieces(start, count):
        result = []
        for j in range(count):
            result += wide(low, high, start + j * half, start + (j + 1) * half)
        return result

    grad_small = (low[:, n_qkv:n_one] + high[:, n_qkv:n_one])[:, :n_small]
    grad_enc = jnp.concatenate(
        pieces(0, 3) + [outs[:rows]] + wide(low, high, n_one, n_two), axis=1
    )
    grad_dec = jnp.concatenate(
        pieces(n_two, 3) + [outs[rows : 2 * rows]] + pieces(n_two + 3 * half, 3)
        + [outs[2 * rows : 3 * rows]] + wide(low, high, n_three, n_three + hid), axis=1
    )
    grad_down = jnp.concatenate(
        [outs[3 * rows : 3 * rows + down_rows], outs[3 * rows + down_rows :]], axis=1
    )

    squares = (
        jnp.sum(grad_enc * grad_enc) + jnp.sum(grad_dec * grad_dec)
        + jnp.sum(grad_down * grad_down) + jnp.sum(grad_small * grad_small)
    )
    squares = jnp.full((8, LANES), squares)
    for axis, pairs_of in (
        ("c", SWAP), ("xl", SWAP), ("xh", SWAP),
        ("y", [(0, 1), (1, 0), (2, 3), (3, 2)]), ("y", [(0, 2), (2, 0), (1, 3), (3, 1)]),
        ("z", [(0, 1), (1, 0), (2, 3), (3, 2)]), ("z", [(0, 2), (2, 0), (1, 3), (3, 1)]),
    ):
        squares = squares + lax.ppermute(squares, axis, pairs_of)
    grad_norm = jnp.sqrt(squares[0, 0])
    factor = CLIP_LEVEL / jnp.maximum(grad_norm, CLIP_LEVEL)
    enc_all = adam_step(enc_master, enc_first, enc_second, grad_enc, factor, RATE_MATRIX, DECAY_RATE)
    dec_all = adam_step(dec_master, dec_first, dec_second, grad_dec, factor, RATE_MATRIX, DECAY_RATE)
    down_all = adam_step(
        down_master, down_first, down_second, grad_down, factor, RATE_MATRIX, DECAY_RATE
    )
    small_all_new = adam_step(
        small_master, small_first, small_second, grad_small, factor, RATE_SMALL, 0.0
    )
    return (
        dec_out[None], src_grad[None], tgt_grad[None], grad_norm,
        enc_all[0], dec_all[0], down_all[0], small_all_new[0],
        enc_all[1], dec_all[1], down_all[1], small_all_new[1],
        enc_all[2], dec_all[2], down_all[2], small_all_new[2],
        grad_small * factor,
    )


def solution(mesh):
    split = Mesh(mesh.devices.reshape(4, 2, 4, 2, 2), ALL_AXES)
    tokens = P(ROW_AXES, POS_AXES, None)
    marks = P(ROW_AXES, POS_AXES)
    shard = P(ALL_AXES, None)
    in_specs = (tokens,) * 3 + (marks,) * 4 + (shard,) * 12
    out_specs = (tokens,) * 3 + (P(),) + (shard,) * 13
    return jax.shard_map(
        per_device, mesh=split, in_specs=in_specs, out_specs=out_specs, check_vma=False
    )
```

time: 2720 us -> 673 us (0.25)
  blocking collectives: 1200 us -> 22.9 us
  local copies, waits for them, and re-layouts: 383 us -> 46.5 us
  starting transfers between devices: 361 us -> 55.6 us
  waiting for transfers between devices: 460 us -> 324 us
  matrix products: 198 us -> 82.2 us
  Pallas kernels: 0 us -> 49.4 us
    unnamed x2 -> x0, blocking collectives: 912 us -> none
    unnamed x67 -> x0, starting transfers between devices: 360 us -> none
    all_gather x6 -> x4, waiting for transfers between devices: 444 us -> 92.3 us  [spread(): return lax.all_gather(shard, ('z', 'y'), axis=0, tiled=True)]
    unnamed x486 -> x465, local copies, waits for them, and re-layouts: 332 us -> 12.2 us
    all_gather x7 -> x2, blocking collectives: 220 us -> 22.9 us  [the longest x1 12.4 us: per_device(): cols = lax.all_gather(cols, ('xh', 'xl'), axis=0, tiled=True)]
    reduce_scatter x4, waiting for transfers between devices: 0.04 us -> 128 us  [reduce(): lax.psum_scatter(jnp.concatenate(parts, axis=1), ('z', 'y'), scatter_dime...]
    dot_general x51, matrix products: 198 us -> 82.2 us  [the longest x18 27.3 us: dot(): return jnp.dot(left, right, preferred_element_type=kind)]
    ppermute x0 -> x49, waiting for transfers between devices: none -> 104 us  [the longest x40 90.2 us: swap(): return lax.ppermute(value, axis, SWAP)]
  transfers between devices with their start and end apart: 77 -> 57, of which waited for: 6 -> 33; matrix products, arithmetic and copies ran while one was open for 54% -> 24% of each run, Pallas kernels for 0% -> 7%
where the time goes in v1:
time: 673 us; the launch traced here: 659 us
  waiting for transfers between devices  324 us (48%)
  matrix products  82.2 us (12%)
  other arithmetic  56.2 us (8%)
  starting transfers between devices  55.6 us (8%)
  Pallas kernels  49.4 us (7%)
  local copies, waits for them, and re-layouts  46.5 us (7%)
  blocking collectives  22.9 us (3%)
  between operations  22.5 us (3%)
    reduce_scatter x4, waiting for transfers between devices, reduce(): lax.psum_scatter(jnp.concatenate(parts, axis=1), ('z', 'y'), scatter_dime...  128 us
    all_gather x4, waiting for transfers between devices, spread(): return lax.all_gather(shard, ('z', 'y'), axis=0, tiled=True)  92.3 us
    ppermute x40, waiting for transfers between devices, swap(): return lax.ppermute(value, axis, SWAP)  90.2 us
    pallas_call x6, Pallas kernels, call_kernel(): pl.pallas_call(kernel, grid=(pairs,), in_specs=in_specs, out_specs=out_sp...  49.4 us
    ppermute x40, starting transfers between devices, swap(): return lax.ppermute(value, axis, SWAP)  33.6 us
    dot_general x18, matrix products, dot(): return jnp.dot(left, right, preferred_element_type=kind)  27.3 us
    dot_general x15, matrix products, dot_t(): lax.dot_general(left, right, (((0,), (0,)), ((), ())), preferred_element_...  27.2 us
    dot_general x17, matrix products, dot_b(): lax.dot_general(left, right, (((1,), (1,)), ((), ())), preferred_element_...  26.4 us
  transfers between devices with their start and end apart: 57, of which 33 were waited for; matrix products, arithmetic and copies ran while one was open for 24% of the time, Pallas kernels for 7%

profile of v1, /device:TPU:1, one launch (start us, length us, event | category | flops | bytes accessed | tf_op | source)
XLA Modules:
  0.0 659.4 jit_solution(8971767332068702963)
XLA Ops:
  12.7 12.4 %all-gather.1 = bf16[4,12,6656]{2,1,0:T(8,128)(2,1)S(1)} all-gather(bf16[1,12,6656]{2,1,0:T(8,128)(2,1)S(1)} %maximum_bitcast_fusion), channel_id=1, replica_groups=mesh['z'=4,'xh'=2,'y'=4,'xl'=2,'c'=2] {'xh','xl'}, dimensions={0}, use_global_device_ids=true | all-gather | bytes 798720 | tf_op jit(solution)/shard_map/all_gather | solution.py:329
  27.1 7.6 %collective-permute-start.2 = (bf16[66,768]{1,0:T(8,128)(2,1)S(1)}, bf16[66,768]{1,0:T(8,128)(2,1)S(1)}, u32[]{:S(2)}, u32[]{:S(2)}) collective-permute-start(bf16[66,768]{1,0:T(8,128)(2,1)S(1)} %fusion.24), channel_id=1, source_target_pairs={{1,64},{64,1},{33,96},{96,33},{3,66},{66,3},{35,98},{98,35},{5,68}... | collective-permute-start | bytes 304136 | tf_op jit(solution)/shard_map/ppermute | solution.py:44
  37.2 10.6 %all-gather.2 = bf16[4,66,768]{2,1,0:T(8,128)(2,1)S(1)} all-gather(bf16[1,66,768]{2,1,0:T(8,128)(2,1)S(1)} %select_bitcast_fusion), channel_id=2, replica_groups=mesh['z'=4,'xh'=2,'y'=4,'xl'=2,'c'=2] {'xh','xl'}, dimensions={0}, use_global_device_ids=true | all-gather | bytes 506880 | tf_op jit(solution)/shard_map/all_gather | solution.py:335
  55.9 18.2 %all-gather.8.cloned.1.call-done = bf16[768,1280]{1,0:T(8,128)(2,1)} async-done(((bf16[48,1280]{1,0:T(8,128)(2,1)}), bf16[768,1280]{1,0:T(8,128)(2,1)}) %all-gather.8.cloned.1.call-update) | async-done | bytes 1966096 | tf_op jit(solution)/shard_map/all_gather | solution.py:354
  86.0 14.6 %collective-permute-done.9.refs_3_.refs_4_ = bf16[512,768]{1,0:T(8,128)(2,1)} collective-permute-done((bf16[512,768]{1,0:T(8,128)(2,1)S(1)}, bf16[512,768]{1,0:T(8,128)(2,1)}, u32[]{:S(2)}, u32[]{:S(2)}) %collective-permute-start.9) | collective-permute-done | bytes 786464 | tf_op jit(solution)/shard_map/ppermute | solution.py:31
  100.6 8.9 %shard_map.342 = (bf16[512,384]{1,0:T(8,128)(2,1)}, f32[3,2,512]{2,1,0:T(2,128)}) custom-call(bf16[512,1152]{1,0:T(8,128)(2,1)} %copy-done.41, bf16[512,1152]{1,0:T(8,128)(2,1)} %copy-done.41, bf16[512,1152]{1,0:T(8,128)(2,1)} %copy-done.41, bf16[512,768]{1,0:T(8,128)(2,1)} %collective-permute-done.9.refs_3_.refs_4_, ...), custom_call_target="tpu_custom_call" | custom-call | flops 3221225472 | bytes 2359296 | tf_op jit(solution)/shard_map/pallas_call | solution.py:225
  109.5 24.1 %all-gather.12.cloned.1.call-done = bf16[768,3456]{1,0:T(8,128)(2,1)} async-done(((bf16[48,3456]{1,0:T(8,128)(2,1)}), bf16[768,3456]{1,0:T(8,128)(2,1)}) %all-gather.12.cloned.1.call-update) | async-done | bytes 5308432 | tf_op jit(solution)/shard_map/all_gather | solution.py:354
  140.1 50.0 %all-gather.10.cloned.1.call-done = bf16[768,3072]{1,0:T(8,128)(2,1)} async-done(((bf16[48,3072]{1,0:T(8,128)(2,1)}), bf16[768,3072]{1,0:T(8,128)(2,1)}) %all-gather.10.cloned.1.call-update) | async-done | bytes 4718608 | tf_op jit(solution)/shard_map/all_gather | solution.py:354
  208.1 5.4 shard_map.341
  225.0 14.1 %collective-permute-done.16.refs_3_.refs_4_ = bf16[512,768]{1,0:T(8,128)(2,1)S(1)} collective-permute-done((bf16[512,768]{1,0:T(8,128)(2,1)S(1)}, bf16[512,768]{1,0:T(8,128)(2,1)S(1)}, u32[]{:S(2)}, u32[]{:S(2)}) %collective-permute-start.16) | collective-permute-done | bytes 786464 | tf_op jit(solution)/shard_map/ppermute | solution.py:31
  240.0 6.9 %shard_map.343 = (bf16[256,384]{1,0:T(8,128)(2,1)}, f32[3,2,256]{2,1,0:T(2,128)}) custom-call(bf16[256,384]{1,0:T(8,128)(2,1)} %fusion.67.refs_0_, bf16[512,768]{1,0:T(8,128)(2,1)} %copy-done.184, bf16[512,768]{1,0:T(8,128)(2,1)} %copy-done.184, bf16[512,768]{1,0:T(8,128)(2,1)} %copy-done.185, bf16[512,768]{1,0:T(8,128)(2,1)} %copy-done.185, ...), custom_call_target="tpu_custom_call" | custom-call | flops 1610612736 | bytes 1966080 | tf_op jit(solution)/shard_map/pallas_call | solution.py:225
  280.1 9.1 %shard_map.344 = (bf16[256,384]{1,0:T(8,128)(2,1)}, f32[512,384]{1,0:T(8,128)}, f32[512,384]{1,0:T(8,128)}, bf16[512,384]{1,0:T(8,128)(2,1)}, bf16[512,384]{1,0:T(8,128)(2,1)}) custom-call(bf16[256,384]{1,0:T(8,128)(2,1)} %fusion.67.refs_0_, bf16[512,768]{1,0:T(8,128)(2,1)} %copy-done.184, bf16[512,768]{1,0:T(8,128)(2,1)} %copy-done.184, ...), custom_call_target="tpu_custom_call" | custom-call | flops 4026531840 | bytes 1966080 | tf_op jit(solution)/shard_map/pallas_call | solution.py:225
  290.7 19.2 %collective-permute-done.23 = bf16[512,768]{1,0:T(8,128)(2,1)S(1)} collective-permute-done((bf16[512,768]{1,0:T(8,128)(2,1)S(1)}, bf16[512,768]{1,0:T(8,128)(2,1)S(1)}, u32[]{:S(2)}, u32[]{:S(2)}) %collective-permute-start.23) | collective-permute-done | bytes 786464 | tf_op jit(solution)/shard_map/ppermute | solution.py:31
  352.1 5.8 shard_map.346
  362.3 7.5 %collective-permute-done.32 = bf16[256,768]{1,0:T(8,128)(2,1)S(1)} collective-permute-done((bf16[256,768]{1,0:T(8,128)(2,1)S(1)}, bf16[256,768]{1,0:T(8,128)(2,1)S(1)}, u32[]{:S(2)}, u32[]{:S(2)}) %collective-permute-start.32) | collective-permute-done | bytes 393248 | tf_op jit(solution)/shard_map/ppermute | solution.py:31
  376.1 13.3 %shard_map.345 = (bf16[512,384]{1,0:T(8,128)(2,1)}, f32[512,384]{1,0:T(8,128)}, f32[512,384]{1,0:T(8,128)}, bf16[512,384]{1,0:T(8,128)(2,1)}, bf16[512,384]{1,0:T(8,128)(2,1)}) custom-call(bf16[512,1152]{1,0:T(8,128)(2,1)} %copy-done.41, bf16[512,1152]{1,0:T(8,128)(2,1)} %copy-done.41, bf16[512,1152]{1,0:T(8,128)(2,1)} %copy-done.41, ...), custom_call_target="tpu_custom_call" | custom-call | flops 8053063680 | bytes 2359296 | tf_op jit(solution)/shard_map/pallas_call | solution.py:225
  399.6 10.5 %collective-permute-done.28 = bf16[512,768]{1,0:T(8,128)(2,1)S(1)} collective-permute-done((bf16[512,768]{1,0:T(8,128)(2,1)S(1)}, bf16[512,768]{1,0:T(8,128)(2,1)S(1)}, u32[]{:S(2)}, u32[]{:S(2)}) %collective-permute-start.28) | collective-permute-done | bytes 786464 | tf_op jit(solution)/shard_map/ppermute | solution.py:31
  461.3 46.4 %reduce-scatter.5.cloned.1.call-done = bf16[48,1280]{1,0:T(8,128)(2,1)} async-done(((bf16[768,1280]{1,0:T(8,128)(2,1)}), bf16[48,1280]{1,0:T(8,128)(2,1)}) %reduce-scatter.5.cloned.1.call-update) | async-done | bytes 122896 | tf_op jit(solution)/shard_map/reduce_scatter | solution.py:501
  507.7 81.5 %reduce-scatter.9.cloned.1.call-done = bf16[48,3072]{1,0:T(8,128)(2,1)} async-done(((bf16[768,3072]{1,0:T(8,128)(2,1)}), bf16[48,3072]{1,0:T(8,128)(2,1)}) %reduce-scatter.9.cloned.1.call-update) | async-done | bytes 294928 | tf_op jit(solution)/shard_map/reduce_scatter | solution.py:501
  594.4 5.5 collective-permute-done.34
  601.2 4.5 collective-permute-done.35
  606.7 4.2 collective-permute-start.36
  611.4 3.7 collective-permute-start.41
  615.9 4.3 collective-permute-done.41
  (875 shorter events, 248.6 us)
Async XLA Ops:
  7.2 66.9 %all-gather.8.cloned.1.call-start = ((), (), s32[]{:S(2)}) async-start(), calls=%async_computation.4 | async-start | bytes 2088960 | tf_op jit(solution)/shard_map/all_gather | solution.py:354
  25.9 107.8 %all-gather.12.cloned.1.call-start = ((), (), s32[]{:S(2)}) async-start(), calls=%async_computation.6 | async-start | bytes 5640192 | tf_op jit(solution)/shard_map/all_gather | solution.py:354
  27.1 10.0 %collective-permute-start.2 = (bf16[66,768]{1,0:T(8,128)(2,1)S(1)}, bf16[66,768]{1,0:T(8,128)(2,1)S(1)}, u32[]{:S(2)}, u32[]{:S(2)}) collective-permute-start(bf16[66,768]{1,0:T(8,128)(2,1)S(1)} %fusion.24), channel_id=1, source_target_pairs={{1,64},{64,1},{33,96},{96,33},{3,66},{66,3},{35,98},{98,35},{5,68}... | collective-permute-start | bytes 304136 | tf_op jit(solution)/shard_map/ppermute | solution.py:44
  48.8 141.3 %all-gather.10.cloned.1.call-start = ((), (), s32[]{:S(2)}) async-start(), calls=%async_computation.5 | async-start | bytes 5013504 | tf_op jit(solution)/shard_map/all_gather | solution.py:354
  49.8 204.1 %all-gather.14.cloned.1.call-start = ((), (), s32[]{:S(2)}) async-start(), calls=%async_computation.7 | async-start | bytes 5013504 | tf_op jit(solution)/shard_map/all_gather | solution.py:354
  53.0 30.2 %collective-permute-start.5 = (s32[256,2]{0,1:T(2,128)S(1)}, s32[256,2]{0,1:T(2,128)S(1)}, u32[]{:S(2)}, u32[]{:S(2)}) collective-permute-start(s32[256,2]{0,1:T(2,128)S(1)} %get-tuple-element.271), channel_id=1, source_target_pairs={{0,2},{2,0},{1,3},{3,1},{4,6},{6,4},{5,7},{7,5},{8,10},{10,8},{9,1... | collective-permute-start | bytes 6152 | tf_op jit(solution)/shard_map/ppermute | solution.py:31
  55.8 28.2 %collective-permute-start.11 = (s32[512,2]{0,1:T(2,128)S(1)}, s32[512,2]{0,1:T(2,128)S(1)}, u32[]{:S(2)}, u32[]{:S(2)}) collective-permute-start(s32[512,2]{0,1:T(2,128)S(1)} %get-tuple-element.251), channel_id=1, source_target_pairs={{0,2},{2,0},{1,3},{3,1},{4,6},{6,4},{5,7},{7,5},{8,10},{10,8},{9,1... | collective-permute-start | bytes 12296 | tf_op jit(solution)/shard_map/ppermute | solution.py:31
  81.3 19.3 %collective-permute-start.9 = (bf16[512,768]{1,0:T(8,128)(2,1)S(1)}, bf16[512,768]{1,0:T(8,128)(2,1)}, u32[]{:S(2)}, u32[]{:S(2)}) collective-permute-start(bf16[512,768]{1,0:T(8,128)(2,1)S(1)} %slice.1029), channel_id=1, source_target_pairs={{0,2},{2,0},{1,3},{3,1},{4,6},{6,4},{5,7},{7,5},{8,10},{10,8},{9,1... | collective-permute-start | bytes 2359304 | tf_op jit(solution)/shard_map/ppermute | solution.py:31
  85.8 361.7 %reduce-scatter.11.cloned.1.call-start = ((), (), s32[]{:S(2)}) async-start(), calls=%async_computation.11 | async-start | bytes 5013504 | tf_op jit(solution)/shard_map/reduce_scatter | solution.py:501
  136.4 59.4 %collective-permute-start.12 = (f32[256,768]{1,0:T(8,128)S(1)}, f32[256,768]{1,0:T(8,128)}, u32[]{:S(2)}, u32[]{:S(2)}) collective-permute-start(f32[256,768]{1,0:T(8,128)S(1)} %slice.1039), channel_id=1, source_target_pairs={{0,1},{1,0},{2,3},{3,2},{4,5},{5,4},{6,7},{7,6},{8,9},{9,8},{10,11... | collective-permute-start | bytes 2359304 | tf_op jit(solution)/shard_map/ppermute | solution.py:31
  192.7 14.6 %collective-permute-start.3 = (bf16[256,768]{1,0:T(8,128)(2,1)S(1)}, bf16[256,768]{1,0:T(8,128)(2,1)S(1)}, u32[]{:S(2)}, u32[]{:S(2)}) collective-permute-start(bf16[256,768]{1,0:T(8,128)(2,1)S(1)} %slice.1009), channel_id=1, source_target_pairs={{0,2},{2,0},{1,3},{3,1},{4,6},{6,4},{5,7},{7,5},{8,10},{10,8},{9,1... | collective-permute-start | bytes 1179656 | tf_op jit(solution)/shard_map/ppermute | solution.py:31
  204.7 10.5 %collective-permute-start.14 = (f32[256,768]{1,0:T(8,128)S(1)}, f32[256,768]{1,0:T(8,128)S(1)}, u32[]{:S(2)}, u32[]{:S(2)}) collective-permute-start(f32[256,768]{1,0:T(8,128)S(1)} %slice.1051), channel_id=1, source_target_pairs={{0,1},{1,0},{2,3},{3,2},{4,5},{5,4},{6,7},{7,6},{8,9},{9,8},{10,11... | collective-permute-start | bytes 2359304 | tf_op jit(solution)/shard_map/ppermute | solution.py:31
  220.2 18.9 %collective-permute-start.16 = (bf16[512,768]{1,0:T(8,128)(2,1)S(1)}, bf16[512,768]{1,0:T(8,128)(2,1)S(1)}, u32[]{:S(2)}, u32[]{:S(2)}) collective-permute-start(bf16[512,768]{1,0:T(8,128)(2,1)S(1)} %add_convert_fusion.refs_1_.refs_2_), channel_id=1, source_target_pairs={{0,2},{2,0},{1,3},{3,1},{4,6},{6,4},{5,7},{7,5},{8,10},{10,8},{9,1... | collective-permute-start | bytes 2359304 | tf_op jit(solution)/shard_map/ppermute | solution.py:31
  272.9 184.1 %reduce-scatter.7.cloned.1.call-start = ((), (), s32[]{:S(2)}) async-start(), calls=%async_computation.9 | async-start | bytes 5849088 | tf_op jit(solution)/shard_map/reduce_scatter | solution.py:501
  290.6 19.3 %collective-permute-start.23 = (bf16[512,768]{1,0:T(8,128)(2,1)S(1)}, bf16[512,768]{1,0:T(8,128)(2,1)S(1)}, u32[]{:S(2)}, u32[]{:S(2)}) collective-permute-start(bf16[512,768]{1,0:T(8,128)(2,1)S(1)} %pad_maximum_fusion.8), channel_id=1, source_target_pairs={{0,2},{2,0},{1,3},{3,1},{4,6},{6,4},{5,7},{7,5},{8,10},{10,8},{9,1... | collective-permute-start | bytes 2359304 | tf_op jit(solution)/shard_map/ppermute | solution.py:31
  341.1 166.6 %reduce-scatter.5.cloned.1.call-start = ((), (), s32[]{:S(2)}) async-start(), calls=%async_computation.8 | async-start | bytes 2088960 | tf_op jit(solution)/shard_map/reduce_scatter | solution.py:501
  359.1 10.7 %collective-permute-start.32 = (bf16[256,768]{1,0:T(8,128)(2,1)S(1)}, bf16[256,768]{1,0:T(8,128)(2,1)S(1)}, u32[]{:S(2)}, u32[]{:S(2)}) collective-permute-start(bf16[256,768]{1,0:T(8,128)(2,1)S(1)} %pad_maximum_fusion.34), channel_id=1, source_target_pairs={{0,2},{2,0},{1,3},{3,1},{4,6},{6,4},{5,7},{7,5},{8,10},{10,8},{9,1... | collective-permute-start | bytes 1179656 | tf_op jit(solution)/shard_map/ppermute | solution.py:31
  373.5 17.5 %collective-permute-start.33 = (f32[128,768]{1,0:T(8,128)S(1)}, f32[128,768]{1,0:T(8,128)S(1)}, u32[]{:S(2)}, u32[]{:S(2)}) collective-permute-start(f32[128,768]{1,0:T(8,128)S(1)} %slice.1094), channel_id=1, source_target_pairs={{0,1},{1,0},{2,3},{3,2},{4,5},{5,4},{6,7},{7,6},{8,9},{9,8},{10,11... | collective-permute-start | bytes 1179656 | tf_op jit(solution)/shard_map/ppermute | solution.py:31
  390.9 19.2 %collective-permute-start.28 = (bf16[512,768]{1,0:T(8,128)(2,1)S(1)}, bf16[512,768]{1,0:T(8,128)(2,1)S(1)}, u32[]{:S(2)}, u32[]{:S(2)}) collective-permute-start(bf16[512,768]{1,0:T(8,128)(2,1)S(1)} %pad_maximum_fusion.11), channel_id=1, source_target_pairs={{0,2},{2,0},{1,3},{3,1},{4,6},{6,4},{5,7},{7,5},{8,10},{10,8},{9,1... | collective-permute-start | bytes 2359304 | tf_op jit(solution)/shard_map/ppermute | solution.py:31
  413.6 9.9 %collective-permute-start.29 = (f32[256,768]{1,0:T(8,128)}, f32[256,768]{1,0:T(8,128)}, u32[]{:S(2)}, u32[]{:S(2)}) collective-permute-start(f32[256,768]{1,0:T(8,128)} %slice.1088), channel_id=1, source_target_pairs={{0,1},{1,0},{2,3},{3,2},{4,5},{5,4},{6,7},{7,6},{8,9},{9,8},{10,11... | collective-permute-start | bytes 2359304 | tf_op jit(solution)/shard_map/ppermute | solution.py:31
  430.6 158.6 %reduce-scatter.9.cloned.1.call-start = ((), (), s32[]{:S(2)}) async-start(), calls=%async_computation.10 | async-start | bytes 5013504 | tf_op jit(solution)/shard_map/reduce_scatter | solution.py:501
  457.9 135.1 %collective-permute-start.37 = (bf16[48,768]{1,0:T(8,128)(2,1)S(1)}, bf16[48,768]{1,0:T(8,128)(2,1)S(1)}, u32[]{:S(2)}, u32[]{:S(2)}) collective-permute-start(bf16[48,768]{1,0:T(8,128)(2,1)S(1)} %broadcast_select_fusion.9), channel_id=1, source_target_pairs={{0,16},{16,0},{1,17},{17,1},{2,18},{18,2},{3,19},{19,3},{4,20},{20... | collective-permute-start | bytes 221192 | tf_op jit(solution)/shard_map/ppermute | solution.py:31
  590.3 9.6 %collective-permute-start.34 = (bf16[24,7808]{1,0:T(8,128)(2,1)S(1)}, bf16[24,7808]{1,0:T(8,128)(2,1)S(1)}, u32[]{:S(2)}, u32[]{:S(2)}) collective-permute-start(bf16[24,7808]{1,0:T(8,128)(2,1)S(1)} %broadcast_select_fusion), channel_id=1, source_target_pairs={{0,16},{16,0},{1,17},{17,1},{2,18},{18,2},{3,19},{19,3},{4,20},{20... | collective-permute-start | bytes 1124360 | tf_op jit(solution)/shard_map/ppermute | solution.py:31
  611.4 8.8 %collective-permute-start.41 = (f32[66,768]{1,0:T(8,128)S(1)}, f32[66,768]{1,0:T(8,128)S(1)}, u32[]{:S(2)}, u32[]{:S(2)}) collective-permute-start(f32[66,768]{1,0:T(8,128)S(1)} %concatenate.317), channel_id=1, source_target_pairs={{1,64},{64,1},{33,96},{96,33},{3,66},{66,3},{35,98},{98,35},{5,68}... | collective-permute-start | bytes 608264 | tf_op jit(solution)/shard_map/ppermute | solution.py:44
  (252 other events, 1807.7 us)
Sparse Core Ops, SparseCore 0:
  26.0 48.0 all-gather.7
  76.8 56.7 all-gather.11
  136.4 53.6 all-gather.9
  192.7 53.8 all-gather.13
  273.0 75.6 reduce-scatter.10
  351.9 79.3 reduce-scatter.6
  434.6 73.0 reduce-scatter.4
  511.4 77.7 reduce-scatter.8

commit v2 on v1

--- a/solution.py
+++ b/solution.py
@@ -31,6 +31,10 @@
     return lax.ppermute(value, axis, SWAP)
 
 
+def flip(value, bits):
+    return lax.ppermute(value, ("xh", "xl"), [(i, i ^ bits) for i in range(4)])
+
+
 def join_core(value):
     return jnp.concatenate([value, swap(value, "c")], axis=0)
 
@@ -40,36 +44,112 @@
     return partial[:mine] + swap(partial[mine:], "c")
 
 
-def swap_z(value):
-    other = lax.ppermute(value, ("z", "c"), [(1, 4), (4, 1), (3, 6), (6, 3)])
-    moved = (lax.axis_index("z") // 2) != lax.axis_index("c")
-    return jnp.where(moved, other, value)
+def move_blocks(sources, specs, outs, steps):
+    n = len(sources)
+
+    def kernel(*refs):
+        sems = refs[-1]
+        copies = [
+            pltpu.make_async_copy(refs[src].at[cut], refs[n + out].at[to], sems.at[j])
+            for j, (src, cut, out, to) in enumerate(steps)
+        ]
+        for copy in copies:
+            copy.start()
+        for copy in copies:
+            copy.wait()
+
+    moved = 2 * sum(o.size * 2 for o in outs)
+    return pl.pallas_call(
+        kernel,
+        grid=(1,),
+        in_specs=specs,
+        out_specs=[pl.BlockSpec(memory_space=pl.ANY)] * len(outs),
+        out_shape=outs,
+        scratch_shapes=[pltpu.SemaphoreType.DMA((len(steps),))],
+        compiler_params=pltpu.CompilerParams(vmem_limit_bytes=56 * 1024 * 1024),
+        cost_estimate=pl.CostEstimate(flops=0, bytes_accessed=moved, transcendentals=0),
+    )(*sources)
+
+
+def spread_down(value, half):
+    n = value.shape[0] // 16
+
+    def plan():
+        steps = []
+        for z in range(4):
+            for y in range(4):
+                for x in range(4):
+                    row = ((((z % 2) * 2 + x // 2) * 4 + y) * 2 + x % 2) * n
+                    stored = (pl.ds((z * 4 + y) * n, n), pl.ds(x * half, half))
+                    own = (pl.ds(row, n), pl.ds((z // 2) * half, half))
+                    steps.append((stored, own))
+        return steps
+
+    return plan()
+
+
+def unpack_down(full, half):
+    rows = full.shape[0]
+    block = jax.ShapeDtypeStruct((rows, 4 * half), BF)
+    steps = [(0, stored, 0, own) for stored, own in spread_down(block, half)]
+    return move_blocks(
+        [full], [pl.BlockSpec((rows, 4 * half), lambda i: (0, 0))],
+        [jax.ShapeDtypeStruct((4 * half, 2 * half), BF)], steps,
+    )[0]
+
+
+def pack_grads(parts, down, half, total):
+    rows = 2 * half
+    sources = [down] + list(parts)
+    steps = [(0, own, 0, stored) for stored, own in spread_down(jax.ShapeDtypeStruct((rows, 4 * half), BF), half)]
+    at = 4 * half
+    for j, part in enumerate(parts):
+        n = part.shape[1]
+        steps.append((j + 1, (slice(None), slice(None)), 0, (slice(None), pl.ds(at, n))))
+        at += n
+    specs = [pl.BlockSpec(s.shape, lambda i: (0, 0)) for s in sources]
+    return move_blocks(sources, specs, [jax.ShapeDtypeStruct((rows, total), BF)], steps)[0]
+
+
+def after(value, *earlier):
+    return lax.optimization_barrier((value,) + earlier)[0]
+
+
+def gather_x(value):
+    here = lax.axis_index("xh") * 2 + lax.axis_index("xl")
+    found = [value] + [flip(value, bits) for bits in (1, 2, 3)]
+    result = []
+    for spot in range(4):
+        part = found[0]
+        for bits in (1, 2, 3):
+            part = jnp.where((here ^ bits) == spot, found[bits], part)
+        result.append(part)
+    return result
+
+
+def gather_by_trade(value, axes, n):
+    return lax.all_to_all(jnp.broadcast_to(value[None], (n,) + value.shape), axes, 0, 0)
+
+
+def sum_by_trade(value, axes):
+    return jnp.sum(lax.all_to_all(value, axes, 0, 0).astype(F32), axis=0)
 
 
 def feature_order(width):
     rest = width // 32
     new = np.arange(width)
     z, y, xh, r = new // (8 * rest), (new // (2 * rest)) % 4, (new // rest) % 2, new % rest
-    old = ((z * 2 + xh) * 4 + y) * rest + r
-    return old
+    return ((z * 2 + xh) * 4 + y) * rest + r
 
 
 def head_order(width):
-    r = width // 128
+    r = width // 64
     own = np.arange(width // 2)
-    z, xh, y, xl, c, i = (
-        own // (32 * r) // 2,
-        (own // (16 * r)) % 2,
-        (own // (4 * r)) % 4,
-        (own // (2 * r)) % 2,
-        (own // r) % 2,
-        own % r,
-    )
-    z = own // (32 * r)
+    zz, xh = own // (16 * r), (own // (8 * r)) % 2
+    y, xl, i = (own // (2 * r)) % 4, (own // r) % 2, own % r
     places = []
-    for half in range(2):
-        place = (((((c * 2 + z) * 4 + y) * 2 + xh) * 2 + xl) * 2 + half) * r + i
-        places.append(place)
+    for cols in range(2):
+        places.append((((cols * 2 + zz) * 4 + y) * 4 + xh * 2 + xl) * r + i)
     return np.concatenate(places)
 
 
@@ -314,9 +394,8 @@
 
     col_blocks = [
         halves(block(encb, 0)), halves(block(encb, 1)), halves(block(encb, 2)), (smallb, smallb),
-        halves(encb[:, 4 * width :]),
-        halves(block(decb, 0)), halves(block(decb, 1)), halves(block(decb, 2)),
-        halves(block(decb, 4)), halves(block(decb, 5)), halves(block(decb, 6)),
+        halves(encb[:, 4 * width :]), halves(block(decb, 5)), halves(block(decb, 6)),
+        halves(block(decb, 0)), halves(block(decb, 1)), halves(block(decb, 2)), halves(block(decb, 4)),
         halves(decb[:, 8 * width :]),
     ]
     cols0 = jnp.concatenate([b[0] for b in col_blocks], axis=1)
@@ -326,36 +405,54 @@
     cols = jnp.concatenate(
         [jnp.where(first_core, mine, theirs), jnp.where(first_core, theirs, mine)], axis=0
     )
-    cols = lax.all_gather(cols, ("xh", "xl"), axis=0, tiled=True)
-
-    row_shard = jnp.concatenate(
-        [block(encb, 3), block(decb, 3), block(decb, 7), downb[:, :width], downb[:, width:]], axis=0
-    )
-    row_shard = swap_z(dot(row_shard, order, BF))
-    row_shard = lax.all_gather(row_shard, ("xh", "xl"), axis=0)
-
-    def pack_out(index):
-        part = row_shard[:, index * rows : (index + 1) * rows].reshape(4, rows, 2, half)
-        return part.transpose(0, 2, 1, 3).reshape(8 * rows, half)
-
-    def pack_down(index):
-        at = 3 * rows + index * down_rows
-        part = row_shard[:, at : at + down_rows].reshape(2, 2 * down_rows, width)
-        return [part[0], part[1]]
-
     n_qkv, n_one = 3 * half, 3 * half + LANES
-    n_two, n_three = n_one + hid, n_one + hid + 6 * half
+    n_two, n_three = n_one + hid + 2 * half, n_one + hid + 6 * half
+    cols = gather_by_trade(cols, ("xh", "xl"), 4).reshape(8 * rows, cols.shape[1])
+
+    z_half = lax.axis_index("z") // 2
+    active = z_half == core
+    row_shard = dot(jnp.concatenate(
+        [block(encb, 3), downb[:, :width], block(decb, 3), block(decb, 7), downb[:, width:]], axis=0
+    ), order, BF)
+    other = swap(row_shard, "c")
+    row_shard = jnp.stack([
+        jnp.where(first_core, row_shard, other), jnp.where(first_core, other, row_shard)
+    ])
+    low, high = row_shard[..., :half], row_shard[..., half:]
+    kept = jnp.where(z_half == 0, low, high)
+    sent = jnp.where(z_half == 0, high, low)
+    row_shard = jnp.where(
+        active, kept, lax.ppermute(sent, ("z", "c"), [(0, 4), (2, 6), (5, 1), (7, 3)])
+    )
+    row_shard = jnp.stack(gather_x(row_shard))
+
+    def pack_out(at):
+        return row_shard[:, :, at : at + rows].reshape(8 * rows, half)
+
+    def pack_down(at):
+        part = row_shard[:, :, at : at + down_rows].reshape(4, 2 * down_rows, half)
+        return [part[j] for j in range(4)]
+
+    dec_rows = rows + down_rows
     shard_one = cols[:, :n_one]
-    shard_two = jnp.concatenate([pack_out(0), cols[:, n_one:n_two]] + pack_down(0), axis=1)
-    shard_three = jnp.concatenate([cols[:, n_two:n_three], pack_out(1), pack_out(2)], axis=1)
-    shard_four = jnp.concatenate([cols[:, n_three:]] + pack_down(1), axis=1)
-
-    def spread(shard):
-        return lax.all_gather(shard, ("z", "y"), axis=0, tiled=True)
-
-    full_one, full_two, full_three, full_four = (
-        spread(shard_one), spread(shard_two), spread(shard_three), spread(shard_four),
-    )
+    shard_two = jnp.concatenate(
+        pack_down(rows) + [cols[:, n_one:n_three]]
+        + [pack_out(0), pack_out(dec_rows), pack_out(dec_rows + rows)], axis=1
+    )
+    shard_three = jnp.concatenate(pack_down(dec_rows + 2 * rows) + [cols[:, n_three:]], axis=1)
+    full_two, full_three = [
+        lax.all_gather(shard, ("z", "y"), axis=0, tiled=True) for shard in (shard_two, shard_three)
+    ]
+    full_one = gather_by_trade(shard_one, ("z", "y"), 16).reshape(width, n_one)
+
+    def cut(full, *counts):
+        starts = [int(v) for v in np.cumsum((hid,) + counts)]
+        return [full[:, a:b] for a, b in zip(starts[:-1], starts[1:])]
+
+    w_eqkv, small_all = full_one[:, :n_qkv], full_one[:, n_qkv:]
+    w_e1, w_ckv, w_dqkv, w_cq, w_eo, w_so, w_co = cut(full_two, hid, 2 * half, n_qkv, half, half, half, half)
+    w_d1 = full_three[:, hid:]
+    w_e2, w_d2 = unpack_down(full_two, half), unpack_down(full_three, half)
 
     def unpack_out(part):
         natural = dot_t(place, part, BF)
@@ -365,27 +462,7 @@
         stacked = jnp.concatenate([grad[:, :half], grad[:, half:]], axis=0)
         return dot(place, stacked, BF)
 
-    def unpack_down(part):
-        part = jnp.stack([part[:, :width], part[:, width:]], axis=0)
-        part = part.reshape(2, 2, 2, 4, 2, down_rows, width)
-        return part.transpose(2, 0, 3, 4, 1, 5, 6).reshape(hid, width)
-
-    def repack_down(grad):
-        part = grad.reshape(2, 2, 4, 2, 2, down_rows, width)
-        part = part.transpose(1, 4, 0, 2, 3, 5, 6).reshape(2, width, width)
-        return [part[0], part[1]]
-
-    w_eqkv, small_all = full_one[:, :n_qkv], full_one[:, n_qkv:]
-    w_eo = unpack_out(full_two[:, :half])
-    w_e1 = full_two[:, half : half + hid]
-    w_e2 = unpack_down(full_two[:, half + hid :])
-    w_dqkv = full_three[:, :n_qkv]
-    w_cq = full_three[:, n_qkv : 4 * half]
-    w_ckv = full_three[:, 4 * half : 6 * half]
-    w_so = unpack_out(full_three[:, 6 * half : 7 * half])
-    w_co = unpack_out(full_three[:, 7 * half :])
-    w_d1 = full_four[:, :hid]
-    w_d2 = unpack_down(full_four[:, hid:])
+    w_eo, w_so, w_co = unpack_out(w_eo), unpack_out(w_so), unpack_out(w_co)
 
     eye = one_hot(np.arange(width), width)
     small_p = dot_t(small_all, eye)
@@ -427,13 +504,13 @@
     enc_att, enc_lse = attend_fwd(False, enc_arrays, src_keys, src_q, pairs)
     enc_one = source + sum_core(dot(enc_att, w_eo)) + small_p[4]
 
-    def feed_fwd(resid, w_in, w_out, base):
+    def feed_fwd(resid, w_in, w_out, small_p, base):
         normed = join_core(norm(resid, small_p[base], small_p[base + 1]))
         active, slope = gelu_parts(dot(normed, w_in) + hidden_bias(base + 3))
         active = active.astype(BF)
         return normed, active, slope, resid + sum_core(dot(active, w_out)) + small_p[base + 2]
 
-    enc_ffn = feed_fwd(enc_one, w_e1, w_e2, 5)
+    enc_ffn = feed_fwd(enc_one, w_e1, w_e2, small_p, 5)
     enc_two = enc_ffn[3]
     memory = join_core(norm(enc_two, small_p[12], small_p[13]))
 
@@ -449,7 +526,7 @@
     cross_arrays = [(cross_q, 0), (cross_kv, 0), (cross_kv, pairs), (cross_far, 0), (cross_far, pairs)]
     cross_att, cross_lse = attend_fwd(False, cross_arrays, src_keys, tgt_q, pairs)
     dec_two = dec_one + sum_core(dot(cross_att, w_co)) + small_p[23]
-    dec_ffn = feed_fwd(dec_two, w_d1, w_d2, 24)
+    dec_ffn = feed_fwd(dec_two, w_d1, w_d2, small_p, 24)
     dec_out = reorder_wide(dec_ffn[3], order)
 
     small_grad = {}
@@ -467,7 +544,7 @@
         for j, part in enumerate((low[:width], low[width:], high[:width], high[width:])):
             own_grad[column + j] = part
 
-    def feed_back(resid, saved, w_in, w_out, base, gradient):
+    def feed_back(resid, saved, w_in, w_out, small_p, base, gradient):
         normed, active, slope = saved[:3]
         branch = gradient.astype(BF)
         small_grad[base + 2] = jnp.sum(branch, axis=0, dtype=F32)
@@ -486,150 +563,146 @@
         branch = join_core(branch)
         return dot_t(attended, branch, BF), dot_b(branch, weight, BF)
 
-    def in_back(resid, normed, grad_proj, weight, column, gradient):
+    def in_back(resid, normed, grad_proj, weight, small_p, column, gradient):
         grad_normed = sum_core(dot_b(grad_proj, weight))
         back, small_grad[column], small_grad[column + 1] = norm_back(
             resid, small_p[column], grad_normed
         )
         return gradient + back, dot_t(normed, grad_proj, BF)
 
-    def gather_back(near_k, near_v, far_k, far_v):
+    def gather_back(near_k, near_v, far_k, far_v, *earlier):
         far = swap(jnp.concatenate([far_k, far_v], axis=1), "xl")
+        far = after(far, *earlier)
         return (jnp.concatenate([near_k, near_v], axis=1) + far).astype(BF)
 
-    def reduce(parts):
-        return lax.psum_scatter(
-            jnp.concatenate(parts, axis=1), ("z", "y"), scatter_dimension=0, tiled=True
-        )
+    def reduce(value):
+        return lax.psum_scatter(value, ("z", "y"), scatter_dimension=0, tiled=True)
 
     top = dot(out_cot[0], order)
-    grad_two, g_d1, g_d2 = feed_back(dec_two, dec_ffn, w_d1, w_d2, 24, top)
-    sum_four = reduce([g_d1] + repack_down(g_d2))
+    grad_two, g_d1, g_d2 = feed_back(dec_two, dec_ffn, w_d1, w_d2, small_p, 24, top)
+    sum_dec = reduce(pack_grads([g_d1], g_d2, half, 2 * hid))
 
     g_co, grad_att = out_back(grad_two, cross_att, w_co, 23)
     cross_gq, ck0, cv0, ck1, cv1 = attend_back(
         False, cross_arrays, grad_att, src_keys, tgt_q, cross_lse
     )
-    cross_gkv = gather_back(ck0, cv0, ck1, cv1)
     put_own(21, jnp.sum(cross_gq, axis=0, dtype=F32))
-    put_own(22, jnp.sum(cross_gkv[:, half:], axis=0, dtype=F32))
-    grad_one, g_cq = in_back(dec_one, cross_norm, cross_gq, w_cq, 19, grad_two)
+    grad_one, g_cq = in_back(dec_one, cross_norm, cross_gq, w_cq, small_p, 19, grad_two)
 
     g_so, grad_att = out_back(grad_one, self_att, w_so, 18)
     self_gq, sk0, sv0, sk1, sv1 = attend_back(True, dec_arrays, grad_att, tgt_keys, tgt_q, self_lse)
+    cross_gkv = gather_back(ck0, cv0, ck1, cv1, self_gq[0, 0])
+    put_own(22, jnp.sum(cross_gkv[:, half:], axis=0, dtype=F32))
     self_grad = jnp.concatenate([self_gq, gather_back(sk0, sv0, sk1, sv1)], axis=1)
     self_sum = jnp.sum(self_grad, axis=0, dtype=F32)
     put_own(16, self_sum[:half])
     put_own(17, self_sum[2 * half :])
-    tgt_grad, g_dqkv = in_back(target, dec_norm, self_grad, w_dqkv, 14, grad_one)
+    tgt_grad, g_dqkv = in_back(target, dec_norm, self_grad, w_dqkv, small_p, 14, grad_one)
     tgt_grad = reorder_wide(tgt_grad, order)
 
     g_ckv = dot_t(memory, cross_gkv, BF)
-    sum_three = reduce([g_dqkv, g_cq, g_ckv, repack_out(g_so), repack_out(g_co)])
     grad_memory = sum_core(dot_b(cross_gkv, w_ckv))
     grad_memory = lax.reduce_precision(grad_memory, 8, 7)
     enc_grad_two, small_grad[12], small_grad[13] = norm_back(enc_two, small_p[12], grad_memory)
 
-    enc_grad_one, g_e1, g_e2 = feed_back(enc_one, enc_ffn, w_e1, w_e2, 5, enc_grad_two)
+    enc_grad_one, g_e1, g_e2 = feed_back(enc_one, enc_ffn, w_e1, w_e2, small_p, 5, enc_grad_two)
     g_eo, grad_att = out_back(enc_grad_one, enc_att, w_eo, 4)
-    spare = jnp.zeros((width, LANES), BF)
-    sum_two = reduce([repack_out(g_eo), g_e1] + repack_down(g_e2) + [spare])
+    rest = [g_e1, g_ckv, g_dqkv, g_cq, repack_out(g_eo), repack_out(g_so), repack_out(g_co)]
+    n_rest = 2 * hid + 9 * half
+    sum_rest = reduce(pack_grads(rest, g_e2, half, n_rest + n_rest % (2 * LANES)))
     enc_gq, ek0, ev0, ek1, ev1 = attend_back(False, enc_arrays, grad_att, src_keys, src_q, enc_lse)
     enc_grad = jnp.concatenate([enc_gq, gather_back(ek0, ev0, ek1, ev1)], axis=1)
     enc_sum = jnp.sum(enc_grad, axis=0, dtype=F32)
     put_own(2, enc_sum[:half])
     put_own(3, enc_sum[2 * half :])
-    src_grad, g_eqkv = in_back(source, enc_norm, enc_grad, w_eqkv, 0, enc_grad_one)
+    src_grad, g_eqkv = in_back(source, enc_norm, enc_grad, w_eqkv, small_p, 0, enc_grad_one)
     src_grad = reorder_wide(src_grad, order)
 
-    empty = jnp.zeros((width,), F32)
-    stored = jnp.stack([small_grad.get(j, empty) for j in range(LANES)]).astype(BF)
-    owned = jnp.stack([own_grad.get(j, empty) for j in range(LANES)]).astype(BF)
-    g_small = (dot_b(eye, stored) + lax.dot_general(
-        order, owned, (((0,), (1,)), ((), ())), preferred_element_type=F32
+    def stacked(rows_of):
+        spot = lax.broadcasted_iota(jnp.int32, (LANES, width), 0)
+        total = jnp.zeros((LANES, width), F32)
+        for column, row in rows_of.items():
+            total = jnp.where(spot == column, row[None], total)
+        return total
+
+    stored, owned = stacked(small_grad), stacked(own_grad)
+    g_small = (dot_b(eye, stored.astype(BF)) + lax.dot_general(
+        order, owned.astype(BF), (((0,), (1,)), ((), ())), preferred_element_type=F32
     )).astype(BF)
-    sum_one = reduce([g_eqkv, g_small])
-
-    xh, xl = lax.axis_index("xh"), lax.axis_index("xl")
+    sum_one = jnp.concatenate([g_eqkv, g_small], axis=1).reshape(16, 8 * rows, n_one)
+    sum_one = sum_by_trade(sum_one, ("z", "y")).astype(BF)
 
     def pick(which, low, high):
-        return jnp.where(which == 0, low, high), jnp.where(which == 0, high, low)
-
-    def sum_x(value):
-        n = value.shape[0] // 2
-        keep, send = pick(xh, value[:n], value[n:])
-        value = keep.astype(F32) + swap(send, "xh").astype(F32)
-        n = n // 2
-        keep, send = pick(xl, value[:n], value[n:])
-        return keep + swap(send.astype(BF), "xl").astype(F32)
-
-    def sum_x_down(value):
-        keep, send = pick(xh, value[:, :width], value[:, width:])
-        value = keep.astype(F32) + swap(send, "xh").astype(F32)
-        keep, send = pick(xl, value[:down_rows], value[down_rows:])
-        return keep + swap(send.astype(BF), "xl").astype(F32)
+        return jnp.where(which, low, high), jnp.where(which, high, low)
 
     def from_cores(value):
-        keep, send = pick(core, value[:rows], value[rows:])
+        keep, send = pick(first_core, value[:rows], value[rows:])
         other = swap(send, "c")
-        return pick(core, keep, other)
+        return pick(first_core, keep, other)
 
     def wide(low, high, start, stop):
         return [jnp.concatenate([low[:, start:stop], high[:, start:stop]], axis=1)]
 
-    def own_columns(shards):
-        shards = swap_z(jnp.concatenate(shards, axis=0))
-        return reorder_wide(shards, order)
-
-    def out_shard(value):
-        return jnp.concatenate([value[:rows], value[rows:]], axis=1)
-
-    cols = sum_x(jnp.concatenate(
-        [sum_one, sum_two[:, : half + hid], sum_three, sum_four[:, :hid]], axis=1
-    ))
-    at_two = n_one + half
-    at_three = at_two + hid
-    at_four = at_three + 8 * half
-    low, high = from_cores(jnp.concatenate(
-        [cols[:, :n_one], cols[:, at_two : at_three + 6 * half], cols[:, at_four:]], axis=1
-    ))
-    outs = own_columns([
-        out_shard(cols[:, n_one:at_two]),
-        out_shard(cols[:, at_three + 6 * half : at_three + 7 * half]),
-        out_shard(cols[:, at_three + 7 * half : at_four]),
-        sum_x_down(sum_two[:, half + hid : half + hid + 2 * width]),
-        sum_x_down(sum_four[:, hid:]),
-    ])
-
-    def pieces(start, count):
+    def pieces(low, high, start, count):
         result = []
         for j in range(count):
             result += wide(low, high, start + j * half, start + (j + 1) * half)
         return result
 
-    grad_small = (low[:, n_qkv:n_one] + high[:, n_qkv:n_one])[:, :n_small]
+    def by_x(part, n_down):
+        return part[:, n_down:].reshape(4, 2 * rows, part.shape[1] - n_down)
+
+    def by_x_down(part):
+        part = part[:, :hid].reshape(4, 2 * rows, 4, half)
+        return part.transpose(2, 1, 0, 3).reshape(4, 2 * rows, hid)
+
+    last = sum_by_trade(jnp.concatenate([
+        by_x(sum_rest[:, :n_rest], hid), by_x(sum_dec, hid), by_x_down(sum_rest), by_x_down(sum_dec),
+        sum_one.reshape(4, 2 * rows, n_one),
+    ], axis=2), ("xh", "xl"))
+    sizes = (hid, 2 * half, n_qkv, half, half, half, half, hid, hid, hid, n_one)
+    starts = [int(v) for v in np.cumsum((0,) + sizes)]
+    s_e1, s_ckv, s_dqkv, s_cq, s_eo, s_so, s_co, s_d1, s_e2, s_d2, s_one = [
+        last[:, a:b] for a, b in zip(starts[:-1], starts[1:])
+    ]
+
+    def down_shard(part):
+        return part.reshape(2 * rows, 4, half).transpose(1, 0, 2).reshape(8 * rows, half)
+
+    by_rows = [s_eo, down_shard(s_e2), s_so, s_co, down_shard(s_d2)]
+    by_rows = jnp.stack([
+        jnp.concatenate([p[: p.shape[0] // 2] for p in by_rows], axis=0),
+        jnp.concatenate([p[p.shape[0] // 2 :] for p in by_rows], axis=0),
+    ])
+    other = lax.ppermute(by_rows, ("z", "c"), [(4, 0), (6, 2), (1, 5), (3, 7)])
+    low, high = pick(z_half == 0, by_rows, other)
+    by_rows = jnp.concatenate([low, high], axis=2)
+    mine = jnp.where(first_core, by_rows[0], by_rows[1])
+    other = swap(jnp.where(first_core, by_rows[1], by_rows[0]), "c")
+    by_rows = jnp.where(active, mine, other)
+    by_rows = reorder_wide(by_rows, order)
+    outs_e, outs_d = by_rows[:dec_rows], by_rows[dec_rows:]
+
+    low, high = from_cores(jnp.concatenate([s_e1, s_ckv, s_dqkv, s_cq, s_d1], axis=1))
+    low_one, high_one = from_cores(s_one)
+
+    grad_small = (low_one[:, n_qkv:] + high_one[:, n_qkv:])[:, :n_small]
     grad_enc = jnp.concatenate(
-        pieces(0, 3) + [outs[:rows]] + wide(low, high, n_one, n_two), axis=1
-    )
+        pieces(low_one, high_one, 0, 3) + [outs_e[:rows]] + wide(low, high, 0, hid), axis=1
+    )
+    at = hid + 2 * half
     grad_dec = jnp.concatenate(
-        pieces(n_two, 3) + [outs[rows : 2 * rows]] + pieces(n_two + 3 * half, 3)
-        + [outs[2 * rows : 3 * rows]] + wide(low, high, n_three, n_three + hid), axis=1
-    )
-    grad_down = jnp.concatenate(
-        [outs[3 * rows : 3 * rows + down_rows], outs[3 * rows + down_rows :]], axis=1
-    )
-
-    squares = (
-        jnp.sum(grad_enc * grad_enc) + jnp.sum(grad_dec * grad_dec)
-        + jnp.sum(grad_down * grad_down) + jnp.sum(grad_small * grad_small)
-    )
+        pieces(low, high, at, 3) + [outs_d[:rows]] + pieces(low, high, at + 3 * half, 1)
+        + pieces(low, high, hid, 2) + [outs_d[rows : 2 * rows]]
+        + wide(low, high, at + 4 * half, at + 4 * half + hid), axis=1
+    )
+    grad_down = jnp.concatenate([outs_e[rows:], outs_d[2 * rows :]], axis=1)
+
+    lasts = last[:, : starts[-2]], s_one[:, :n_qkv], grad_small
+    squares = sum(jnp.sum(part * part) for part in lasts)
     squares = jnp.full((8, LANES), squares)
-    for axis, pairs_of in (
-        ("c", SWAP), ("xl", SWAP), ("xh", SWAP),
-        ("y", [(0, 1), (1, 0), (2, 3), (3, 2)]), ("y", [(0, 2), (2, 0), (1, 3), (3, 1)]),
-        ("z", [(0, 1), (1, 0), (2, 3), (3, 2)]), ("z", [(0, 2), (2, 0), (1, 3), (3, 1)]),
-    ):
-        squares = squares + lax.ppermute(squares, axis, pairs_of)
+    squares = squares + swap(squares, "c")
+    squares = jnp.sum(gather_by_trade(squares, ("z", "xh", "y", "xl"), 64), axis=0)
     grad_norm = jnp.sqrt(squares[0, 0])
     factor = CLIP_LEVEL / jnp.maximum(grad_norm, CLIP_LEVEL)
     enc_all = adam_step(enc_master, enc_first, enc_second, grad_enc, factor, RATE_MATRIX, DECAY_RATE)

time: 673 us -> 506 us (0.75)
  waiting for transfers between devices: 324 us -> 186 us
  blocking collectives: 22.9 us -> 0 us
  Pallas kernels: 49.4 us -> 70.1 us
  local copies, waits for them, and re-layouts: 46.5 us -> 28.6 us
  other arithmetic: 56.2 us -> 43.8 us
    reduce_scatter x4 -> x2, waiting for transfers between devices: 128 us -> 7.64 us  [reduce(): return lax.psum_scatter(value, ('z', 'y'), scatter_dimension=0, tiled=True)]
    all_to_all x0 -> x5, waiting for transfers between devices: none -> 96.5 us  [the longest x3 55.1 us: gather_by_trade(): lax.all_to_all(jnp.broadcast_to(value[None], (n,) + value.shape), axes, 0...]
    all_gather x4 -> x2, waiting for transfers between devices: 92.3 us -> 9.4 us  [per_device(): lax.all_gather(shard, ('z', 'y'), axis=0, tiled=True)]
    all_to_all x0 -> x5, starting transfers between devices: none -> 25.1 us  [the longest x3 15.8 us: gather_by_trade(): lax.all_to_all(jnp.broadcast_to(value[None], (n,) + value.shape), axes, 0...]
    ppermute x40 -> x38, waiting for transfers between devices: 90.2 us -> 66.4 us  [swap(): return lax.ppermute(value, axis, SWAP)]
    all_gather x2 -> x0, blocking collectives: 22.9 us -> none  [the longest x1 12.4 us: per_device(): cols = lax.all_gather(cols, ('xh', 'xl'), axis=0, tiled=True)]
    pallas_call x0 -> x4, Pallas kernels: none -> 21 us  [move_blocks(): pl.pallas_call(kernel, grid=(1,), in_specs=specs, out_specs=[pl.BlockSpec...]
    another operation x41 -> x1, local copies, waits for them, and re-layouts: 18.9 us -> 0.01 us  [the longest x15 9.29 us: per_device(): owned = jnp.stack([own_grad.get(j, empty) for j in range(LANES)]).astype(BF)]
  transfers between devices with their start and end apart: 57 -> 52, of which waited for: 33 -> 19; matrix products, arithmetic and copies ran while one was open for 24% -> 25% of each run, Pallas kernels for 7% -> 14%
where the time goes in v2:
time: 506 us; the launch traced here: 497 us
  waiting for transfers between devices  186 us (37%)
  matrix products  87.3 us (17%)
  Pallas kernels  70.1 us (14%)
  starting transfers between devices  60.4 us (12%)
  other arithmetic  43.8 us (9%)
  local copies, waits for them, and re-layouts  28.6 us (6%)
  between operations  21.2 us (4%)
    ppermute x38, waiting for transfers between devices, swap(): return lax.ppermute(value, axis, SWAP)  66.4 us
    all_to_all x3, waiting for transfers between devices, gather_by_trade(): lax.all_to_all(jnp.broadcast_to(value[None], (n,) + value.shape), axes, 0...  55.1 us
    pallas_call x6, Pallas kernels, call_kernel(): pl.pallas_call(kernel, grid=(pairs,), in_specs=in_specs, out_specs=out_sp...  49.1 us
    all_to_all x2, waiting for transfers between devices, sum_by_trade(): return jnp.sum(lax.all_to_all(value, axes, 0, 0).astype(F32), axis=0)  41.3 us
    dot_general x18, matrix products, dot(): return jnp.dot(left, right, preferred_element_type=kind)  31.1 us
    dot_general x15, matrix products, dot_t(): lax.dot_general(left, right, (((0,), (0,)), ((), ())), preferred_element_...  27.7 us
    dot_general x17, matrix products, dot_b(): lax.dot_general(left, right, (((1,), (1,)), ((), ())), preferred_element_...  27.6 us
    ppermute x38, starting transfers between devices, swap(): return lax.ppermute(value, axis, SWAP)  26.4 us
  transfers between devices with their start and end apart: 52, of which 19 were waited for; matrix products, arithmetic and copies ran while one was open for 25% of the time, Pallas kernels for 14%

profile of v2, /device:TPU:1, one launch (start us, length us, event | category | flops | bytes accessed | tf_op | source)
XLA Modules:
  0.0 497.2 jit_solution(15418268144840642456)
XLA Ops:
  15.9 5.8 %collective-permute-done.3 = bf16[2,66,384]{2,1,0:T(8,128)(2,1)S(1)} collective-permute-done((bf16[2,66,384]{2,1,0:T(8,128)(2,1)S(1)}, bf16[2,66,384]{2,1,0:T(8,128)(2,1)S(1)}, u32[]{:S(2)}, u32[]{:S(2)}) %collective-permute-start.3) | collective-permute-done | bytes 101408 | tf_op jit(solution)/shard_map/ppermute | solution.py:425
  30.7 9.6 %all-to-all-done = bf16[4,12,6656]{2,1,0:T(8,128)(2,1)S(1)} async-done(((bf16[4,12,6656]{2,1,0:T(8,128)(2,1)}), bf16[4,12,6656]{2,1,0:T(8,128)(2,1)S(1)}, u32[]{:S(2)}, u32[]{:S(2)}) %all-to-all-start) | async-done | bytes 639008 | tf_op jit(solution)/shard_map/all_to_all | solution.py:131
  48.3 6.4 %all-to-all-start.1 = ((bf16[16,48,1280]{2,1,0:T(8,128)(2,1)}), bf16[16,48,1280]{2,1,0:T(8,128)(2,1)}, u32[]{:S(2)}, u32[]{:S(2)}) async-start(bf16[16,48,1280]{2,1,0:T(8,128)(2,1)} %broadcast_in_dim.273), calls=%async_computation.1 | async-start | bytes 3932160 | tf_op jit(solution)/shard_map/all_to_all | solution.py:131
  57.5 36.7 %all-to-all-done.1 = bf16[16,48,1280]{2,1,0:T(8,128)(2,1)} async-done(((bf16[16,48,1280]{2,1,0:T(8,128)(2,1)}), bf16[16,48,1280]{2,1,0:T(8,128)(2,1)}, u32[]{:S(2)}, u32[]{:S(2)}) %all-to-all-start.1) | async-done | bytes 1966112 | tf_op jit(solution)/shard_map/all_to_all | solution.py:131
  106.7 15.9 %collective-permute-done.13.refs_3_.refs_4_ = bf16[512,768]{1,0:T(8,128)(2,1)} collective-permute-done((bf16[512,768]{1,0:T(8,128)(2,1)S(1)}, bf16[512,768]{1,0:T(8,128)(2,1)}, u32[]{:S(2)}, u32[]{:S(2)}) %collective-permute-start.13) | collective-permute-done | bytes 786464 | tf_op jit(solution)/shard_map/ppermute | solution.py:31
  122.6 8.8 %shard_map.342 = (bf16[512,384]{1,0:T(8,128)(2,1)}, f32[3,2,512]{2,1,0:T(2,128)}) custom-call(bf16[512,1152]{1,0:T(8,128)(2,1)} %copy-done.33, bf16[512,1152]{1,0:T(8,128)(2,1)} %copy-done.33, bf16[512,1152]{1,0:T(8,128)(2,1)} %copy-done.33, bf16[512,768]{1,0:T(8,128)(2,1)} %collective-permute-done.13.refs_3_.refs_4_, ...), custom_call_target="tpu_custom_call" | custom-call | flops 3221225472 | bytes 2359296 | tf_op jit(solution)/shard_map/pallas_call | solution.py:305
  131.4 9.4 %all-gather.3.cloned.1.call-done.refs_0_ = bf16[768,6528]{1,0:T(8,128)(2,1)} async-done(((bf16[48,6528]{1,0:T(8,128)(2,1)}), bf16[768,6528]{1,0:T(8,128)(2,1)}) %all-gather.3.cloned.1.call-update) | async-done | bytes 10027024 | tf_op jit(solution)/shard_map/all_gather | solution.py:444
  159.4 5.1 %multiply_convert_fusion = (bf16[512,1536]{1,0:T(8,128)(2,1)S(1)}, f32[512,1536]{1,0:T(8,128)}) fusion(f32[1536]{0:T(1024)S(1)} %maximum_select_fusion, bf16[768,6528]{1,0:T(8,128)(2,1)} %all-gather.3.cloned.1.call-done.refs_0_, bf16[256,768]{1,0:T(8,128)(2,1)S(1)} %collective-permute-done.17, bf16[256,768]{1,0:T(8,128)(2,1)S(1)} %add_convert_fusion.2), kind=kOutput, calls=%fused_computation.9 | convolution fusion | flops 1214251008 | bytes 7870464 | tf_op jit(solution)/shard_map/dot_general | solution.py:162
  169.9 5.4 %shard_map.341 = (bf16[256,384]{1,0:T(8,128)(2,1)}, f32[3,2,256]{2,1,0:T(2,128)}) custom-call(bf16[256,1152]{1,0:T(8,128)(2,1)} %copy-done.49, bf16[256,1152]{1,0:T(8,128)(2,1)} %copy-done.49, bf16[256,1152]{1,0:T(8,128)(2,1)} %copy-done.49, bf16[256,768]{1,0:T(8,128)(2,1)} %collective-permute-done.7.refs_3_.refs_4_, ...), custom_call_target="tpu_custom_call" | custom-call | flops 805306368 | bytes 1179648 | tf_op jit(solution)/shard_map/pallas_call | solution.py:305
  186.6 14.5 %collective-permute-done.20.refs_3_.refs_4_ = bf16[512,768]{1,0:T(8,128)(2,1)S(1)} collective-permute-done((bf16[512,768]{1,0:T(8,128)(2,1)S(1)}, bf16[512,768]{1,0:T(8,128)(2,1)S(1)}, u32[]{:S(2)}, u32[]{:S(2)}) %collective-permute-start.20) | collective-permute-done | bytes 786464 | tf_op jit(solution)/shard_map/ppermute | solution.py:31
  202.1 6.8 %shard_map.344 = (bf16[256,384]{1,0:T(8,128)(2,1)}, f32[3,2,256]{2,1,0:T(2,128)}) custom-call(bf16[256,384]{1,0:T(8,128)(2,1)} %fusion.64.refs_0_, bf16[512,768]{1,0:T(8,128)(2,1)} %copy-done.122, bf16[512,768]{1,0:T(8,128)(2,1)} %copy-done.122, bf16[512,768]{1,0:T(8,128)(2,1)} %copy-done.123, bf16[512,768]{1,0:T(8,128)(2,1)} %copy-done.123, ...), custom_call_target="tpu_custom_call" | custom-call | flops 1610612736 | bytes 1966080 | tf_op jit(solution)/shard_map/pallas_call | solution.py:305
  238.4 5.2 %shard_map.350 = bf16[768,3072]{1,0:T(8,128)(2,1)} custom-call(bf16[1536,768]{1,0:T(8,128)(2,1)} %fusion.129.refs_0_, bf16[768,1536]{1,0:T(8,128)(2,1)} %fusion.130.refs_1_), custom_call_target="tpu_custom_call" | custom-call | bytes 9437184 | tf_op jit(solution)/shard_map/pallas_call | solution.py:62
  246.7 9.0 %shard_map.346 = (bf16[256,384]{1,0:T(8,128)(2,1)}, f32[512,384]{1,0:T(8,128)}, f32[512,384]{1,0:T(8,128)}, bf16[512,384]{1,0:T(8,128)(2,1)}, bf16[512,384]{1,0:T(8,128)(2,1)}) custom-call(bf16[256,384]{1,0:T(8,128)(2,1)} %fusion.64.refs_0_, bf16[512,768]{1,0:T(8,128)(2,1)} %copy-done.122, bf16[512,768]{1,0:T(8,128)(2,1)} %copy-done.122, ...), custom_call_target="tpu_custom_call" | custom-call | flops 4026531840 | bytes 1966080 | tf_op jit(solution)/shard_map/pallas_call | solution.py:305
  262.8 13.3 %collective-permute-done.27 = bf16[512,768]{1,0:T(8,128)(2,1)S(1)} collective-permute-done((bf16[512,768]{1,0:T(8,128)(2,1)S(1)}, bf16[512,768]{1,0:T(8,128)(2,1)S(1)}, u32[]{:S(2)}, u32[]{:S(2)}) %collective-permute-start.27) | collective-permute-done | bytes 786464 | tf_op jit(solution)/shard_map/ppermute | solution.py:31
  284.7 5.8 %shard_map.348 = (bf16[256,384]{1,0:T(8,128)(2,1)}, f32[256,384]{1,0:T(8,128)}, f32[256,384]{1,0:T(8,128)}, bf16[256,384]{1,0:T(8,128)(2,1)}, bf16[256,384]{1,0:T(8,128)(2,1)}) custom-call(bf16[256,1152]{1,0:T(8,128)(2,1)} %copy-done.49, bf16[256,1152]{1,0:T(8,128)(2,1)} %copy-done.49, bf16[256,1152]{1,0:T(8,128)(2,1)} %copy-done.49, ...), custom_call_target="tpu_custom_call" | custom-call | flops 2013265920 | bytes 1179648 | tf_op jit(solution)/shard_map/pallas_call | solution.py:305
  319.2 8.3 %shard_map.349 = bf16[768,6656]{1,0:T(8,128)(2,1)} custom-call(bf16[1536,768]{1,0:T(8,128)(2,1)} %fusion.99.refs_0_, bf16[768,1536]{1,0:T(8,128)(2,1)} %fusion.101.refs_1_, bf16[768,768]{1,0:T(8,128)(2,1)} %fusion.100.refs_2_, bf16[768,1152]{1,0:T(8,128)(2,1)} %fusion.132.refs_3_, bf16[768,384]{1,0:T(8,128)(2,1)} %fusion.131.refs_4_, ...), custom_call_target="tpu_custom_call" | custom-call | bytes 20447232 | tf_op jit(solution)/shard_map/pallas_call | solution.py:62
  334.7 13.3 %shard_map.347 = (bf16[512,384]{1,0:T(8,128)(2,1)}, f32[512,384]{1,0:T(8,128)}, f32[512,384]{1,0:T(8,128)}, bf16[512,384]{1,0:T(8,128)(2,1)}, bf16[512,384]{1,0:T(8,128)(2,1)}) custom-call(bf16[512,1152]{1,0:T(8,128)(2,1)} %copy-done.33, bf16[512,1152]{1,0:T(8,128)(2,1)} %copy-done.33, bf16[512,1152]{1,0:T(8,128)(2,1)} %copy-done.33, ...), custom_call_target="tpu_custom_call" | custom-call | flops 8053063680 | bytes 2359296 | tf_op jit(solution)/shard_map/pallas_call | solution.py:305
  352.2 16.5 %collective-permute-done.32 = bf16[512,768]{1,0:T(8,128)(2,1)S(1)} collective-permute-done((bf16[512,768]{1,0:T(8,128)(2,1)S(1)}, bf16[512,768]{1,0:T(8,128)(2,1)S(1)}, u32[]{:S(2)}, u32[]{:S(2)}) %collective-permute-start.32) | collective-permute-done | bytes 786464 | tf_op jit(solution)/shard_map/ppermute | solution.py:31
  380.2 5.2 %all-to-all-start.2 = ((bf16[16,48,1280]{2,1,0:T(8,128)(2,1)}), bf16[16,48,1280]{2,1,0:T(8,128)(2,1)S(1)}, u32[]{:S(2)}, u32[]{:S(2)}) async-start(bf16[16,48,1280]{2,1,0:T(8,128)(2,1)} %bitcast.148), calls=%async_computation.4 | async-start | bytes 3932160 | tf_op jit(solution)/shard_map/all_to_all | solution.py:135
  390.5 27.3 %all-to-all-done.2 = bf16[16,48,1280]{2,1,0:T(8,128)(2,1)S(1)} async-done(((bf16[16,48,1280]{2,1,0:T(8,128)(2,1)}), bf16[16,48,1280]{2,1,0:T(8,128)(2,1)S(1)}, u32[]{:S(2)}, u32[]{:S(2)}) %all-to-all-start.2) | async-done | bytes 1966112 | tf_op jit(solution)/shard_map/all_to_all | solution.py:135
  419.4 7.6 %reduce-scatter.3.cloned.1.call-done = bf16[48,6656]{1,0:T(8,128)(2,1)} async-done(((bf16[768,6656]{1,0:T(8,128)(2,1)}), bf16[48,6656]{1,0:T(8,128)(2,1)}) %reduce-scatter.3.cloned.1.call-update) | async-done | bytes 638992 | tf_op jit(solution)/shard_map/reduce_scatter | solution.py:579
  439.7 14.0 %all-to-all-done.3 = bf16[4,12,10880]{2,1,0:T(8,128)(2,1)S(1)} async-done(((bf16[4,12,10880]{2,1,0:T(8,128)(2,1)}), bf16[4,12,10880]{2,1,0:T(8,128)(2,1)S(1)}, u32[]{:S(2)}, u32[]{:S(2)}) %all-to-all-start.3) | async-done | bytes 1044512 | tf_op jit(solution)/shard_map/all_to_all | solution.py:135
  467.9 5.4 %all-to-all-start.4 = ((f32[64,8,128]{2,1,0:T(8,128)}), f32[64,8,128]{2,1,0:T(8,128)S(1)}, u32[]{:S(2)}, u32[]{:S(2)}) async-start(f32[64,8,128]{2,1,0:T(8,128)} %broadcast_in_dim.311), calls=%async_computation.6 | async-start | bytes 524288 | tf_op jit(solution)/shard_map/all_to_all | solution.py:131
  474.2 8.8 %all-to-all-done.4 = f32[64,8,128]{2,1,0:T(8,128)S(1)} async-done(((f32[64,8,128]{2,1,0:T(8,128)}), f32[64,8,128]{2,1,0:T(8,128)S(1)}, u32[]{:S(2)}, u32[]{:S(2)}) %all-to-all-start.4) | async-done | bytes 262176 | tf_op jit(solution)/shard_map/all_to_all | solution.py:131
  (719 shorter events, 211.9 us)
Async XLA Ops:
  26.1 14.2 %all-to-all-start = ((bf16[4,12,6656]{2,1,0:T(8,128)(2,1)}), bf16[4,12,6656]{2,1,0:T(8,128)(2,1)S(1)}, u32[]{:S(2)}, u32[]{:S(2)}) async-start(bf16[4,12,6656]{2,1,0:T(8,128)(2,1)} %broadcast_in_dim.272), calls=%async_computation | async-start | bytes 1703936 | tf_op jit(solution)/shard_map/all_to_all | solution.py:131
  30.1 110.8 %all-gather.3.cloned.1.call-start = ((), (), s32[]{:S(2)}) async-start(), calls=%async_computation.7 | async-start | bytes 10653696 | tf_op jit(solution)/shard_map/all_gather | solution.py:444
  41.4 13.8 %collective-permute-start.8 = (s32[128,3]{0,1:T(4,128)S(1)}, s32[128,3]{0,1:T(4,128)S(1)}, u32[]{:S(2)}, u32[]{:S(2)}) collective-permute-start(s32[128,3]{0,1:T(4,128)S(1)} %pad_add_fusion.6), channel_id=1, source_target_pairs={{0,1},{1,0},{2,3},{3,2},{4,5},{5,4},{6,7},{7,6},{8,9},{9,8},{10,11... | collective-permute-start | bytes 4616 | tf_op jit(solution)/shard_map/ppermute | solution.py:31
  45.3 10.8 %collective-permute-start.14 = (s32[256,3]{0,1:T(4,128)S(1)}, s32[256,3]{0,1:T(4,128)S(1)}, u32[]{:S(2)}, u32[]{:S(2)}) collective-permute-start(s32[256,3]{0,1:T(4,128)S(1)} %pad_add_fusion.4), channel_id=1, source_target_pairs={{0,1},{1,0},{2,3},{3,2},{4,5},{5,4},{6,7},{7,6},{8,9},{9,8},{10,11... | collective-permute-start | bytes 9224 | tf_op jit(solution)/shard_map/ppermute | solution.py:31
  48.3 45.9 %all-to-all-start.1 = ((bf16[16,48,1280]{2,1,0:T(8,128)(2,1)}), bf16[16,48,1280]{2,1,0:T(8,128)(2,1)}, u32[]{:S(2)}, u32[]{:S(2)}) async-start(bf16[16,48,1280]{2,1,0:T(8,128)(2,1)} %broadcast_in_dim.273), calls=%async_computation.1 | async-start | bytes 3932160 | tf_op jit(solution)/shard_map/all_to_all | solution.py:131
  54.6 162.5 %all-gather.5.cloned.1.call-start = ((), (), s32[]{:S(2)}) async-start(), calls=%async_computation.8 | async-start | bytes 5013504 | tf_op jit(solution)/shard_map/all_gather | solution.py:444
  55.2 49.5 %collective-permute-start.9 = (s32[256,2]{0,1:T(2,128)S(1)}, s32[256,2]{0,1:T(2,128)S(1)}, u32[]{:S(2)}, u32[]{:S(2)}) collective-permute-start(s32[256,2]{0,1:T(2,128)S(1)} %get-tuple-element.272), channel_id=1, source_target_pairs={{0,2},{2,0},{1,3},{3,1},{4,6},{6,4},{5,7},{7,5},{8,10},{10,8},{9,1... | collective-permute-start | bytes 6152 | tf_op jit(solution)/shard_map/ppermute | solution.py:31
  56.2 49.4 %collective-permute-start.15 = (s32[512,2]{0,1:T(2,128)S(1)}, s32[512,2]{0,1:T(2,128)S(1)}, u32[]{:S(2)}, u32[]{:S(2)}) collective-permute-start(s32[512,2]{0,1:T(2,128)S(1)} %get-tuple-element.252), channel_id=1, source_target_pairs={{0,2},{2,0},{1,3},{3,1},{4,6},{6,4},{5,7},{7,5},{8,10},{10,8},{9,1... | collective-permute-start | bytes 12296 | tf_op jit(solution)/shard_map/ppermute | solution.py:31
  103.1 19.5 %collective-permute-start.13 = (bf16[512,768]{1,0:T(8,128)(2,1)S(1)}, bf16[512,768]{1,0:T(8,128)(2,1)}, u32[]{:S(2)}, u32[]{:S(2)}) collective-permute-start(bf16[512,768]{1,0:T(8,128)(2,1)S(1)} %slice.1053), channel_id=1, source_target_pairs={{0,2},{2,0},{1,3},{3,1},{4,6},{6,4},{5,7},{7,5},{8,10},{10,8},{9,1... | collective-permute-start | bytes 2359304 | tf_op jit(solution)/shard_map/ppermute | solution.py:31
  146.1 272.1 %reduce-scatter.5.cloned.1.call-start = ((), (), s32[]{:S(2)}) async-start(), calls=%async_computation.10 | async-start | bytes 5013504 | tf_op jit(solution)/shard_map/reduce_scatter | solution.py:579
  152.4 17.4 %collective-permute-start.7 = (bf16[256,768]{1,0:T(8,128)(2,1)S(1)}, bf16[256,768]{1,0:T(8,128)(2,1)}, u32[]{:S(2)}, u32[]{:S(2)}) collective-permute-start(bf16[256,768]{1,0:T(8,128)(2,1)S(1)} %slice.1033), channel_id=1, source_target_pairs={{0,2},{2,0},{1,3},{3,1},{4,6},{6,4},{5,7},{7,5},{8,10},{10,8},{9,1... | collective-permute-start | bytes 1179656 | tf_op jit(solution)/shard_map/ppermute | solution.py:31
  182.2 18.9 %collective-permute-start.20 = (bf16[512,768]{1,0:T(8,128)(2,1)S(1)}, bf16[512,768]{1,0:T(8,128)(2,1)S(1)}, u32[]{:S(2)}, u32[]{:S(2)}) collective-permute-start(bf16[512,768]{1,0:T(8,128)(2,1)S(1)} %add_convert_fusion.refs_1_.refs_2_), channel_id=1, source_target_pairs={{0,2},{2,0},{1,3},{3,1},{4,6},{6,4},{5,7},{7,5},{8,10},{10,8},{9,1... | collective-permute-start | bytes 2359304 | tf_op jit(solution)/shard_map/ppermute | solution.py:31
  243.6 183.5 %reduce-scatter.3.cloned.1.call-start = ((), (), s32[]{:S(2)}) async-start(), calls=%async_computation.9 | async-start | bytes 10862592 | tf_op jit(solution)/shard_map/reduce_scatter | solution.py:579
  256.9 19.2 %collective-permute-start.27 = (bf16[512,768]{1,0:T(8,128)(2,1)S(1)}, bf16[512,768]{1,0:T(8,128)(2,1)S(1)}, u32[]{:S(2)}, u32[]{:S(2)}) collective-permute-start(bf16[512,768]{1,0:T(8,128)(2,1)S(1)} %pad_maximum_fusion.5), channel_id=1, source_target_pairs={{0,2},{2,0},{1,3},{3,1},{4,6},{6,4},{5,7},{7,5},{8,10},{10,8},{9,1... | collective-permute-start | bytes 2359304 | tf_op jit(solution)/shard_map/ppermute | solution.py:31
  278.7 13.1 %collective-permute-start.28 = (f32[256,768]{1,0:T(8,128)S(1)}, f32[256,768]{1,0:T(8,128)S(1)}, u32[]{:S(2)}, u32[]{:S(2)}) collective-permute-start(f32[256,768]{1,0:T(8,128)S(1)} %slice.1102), channel_id=1, source_target_pairs={{0,1},{1,0},{2,3},{3,2},{4,5},{5,4},{6,7},{7,6},{8,9},{9,8},{10,11... | collective-permute-start | bytes 2359304 | tf_op jit(solution)/shard_map/ppermute | solution.py:31
  291.6 13.5 %collective-permute-start.36 = (bf16[256,768]{1,0:T(8,128)(2,1)S(1)}, bf16[256,768]{1,0:T(8,128)(2,1)S(1)}, u32[]{:S(2)}, u32[]{:S(2)}) collective-permute-start(bf16[256,768]{1,0:T(8,128)(2,1)S(1)} %pad_maximum_fusion.29), channel_id=1, source_target_pairs={{0,2},{2,0},{1,3},{3,1},{4,6},{6,4},{5,7},{7,5},{8,10},{10,8},{9,1... | collective-permute-start | bytes 1179656 | tf_op jit(solution)/shard_map/ppermute | solution.py:31
  332.5 18.2 %collective-permute-start.37 = (f32[128,768]{1,0:T(8,128)S(1)}, f32[128,768]{1,0:T(8,128)S(1)}, u32[]{:S(2)}, u32[]{:S(2)}) collective-permute-start(f32[128,768]{1,0:T(8,128)S(1)} %slice.1112), channel_id=1, source_target_pairs={{0,1},{1,0},{2,3},{3,2},{4,5},{5,4},{6,7},{7,6},{8,9},{9,8},{10,11... | collective-permute-start | bytes 1179656 | tf_op jit(solution)/shard_map/ppermute | solution.py:31
  349.4 19.3 %collective-permute-start.32 = (bf16[512,768]{1,0:T(8,128)(2,1)S(1)}, bf16[512,768]{1,0:T(8,128)(2,1)S(1)}, u32[]{:S(2)}, u32[]{:S(2)}) collective-permute-start(bf16[512,768]{1,0:T(8,128)(2,1)S(1)} %pad_maximum_fusion.8), channel_id=1, source_target_pairs={{0,2},{2,0},{1,3},{3,1},{4,6},{6,4},{5,7},{7,5},{8,10},{10,8},{9,1... | collective-permute-start | bytes 2359304 | tf_op jit(solution)/shard_map/ppermute | solution.py:31
  380.2 37.6 %all-to-all-start.2 = ((bf16[16,48,1280]{2,1,0:T(8,128)(2,1)}), bf16[16,48,1280]{2,1,0:T(8,128)(2,1)S(1)}, u32[]{:S(2)}, u32[]{:S(2)}) async-start(bf16[16,48,1280]{2,1,0:T(8,128)(2,1)} %bitcast.148), calls=%async_computation.4 | async-start | bytes 3932160 | tf_op jit(solution)/shard_map/all_to_all | solution.py:135
  432.2 21.6 %all-to-all-start.3 = ((bf16[4,12,10880]{2,1,0:T(8,128)(2,1)}), bf16[4,12,10880]{2,1,0:T(8,128)(2,1)S(1)}, u32[]{:S(2)}, u32[]{:S(2)}) async-start(bf16[4,12,10880]{2,1,0:T(8,128)(2,1)} %constant_dynamic-update-slice_fusion.35), calls=%async_computation.5 | async-start | bytes 2785280 | tf_op jit(solution)/shard_map/all_to_all | solution.py:135
  457.9 15.5 %collective-permute-start.42 = (f32[6,5376]{1,0:T(8,128)S(1)}, f32[6,5376]{1,0:T(8,128)S(1)}, u32[]{:S(2)}, u32[]{:S(2)}) collective-permute-start(f32[6,5376]{1,0:T(8,128)S(1)} %broadcast_select_fusion.9), channel_id=1, source_target_pairs={{0,1},{1,0},{2,3},{3,2},{4,5},{5,4},{6,7},{7,6},{8,9},{9,8},{10,11... | collective-permute-start | bytes 387080 | tf_op jit(solution)/shard_map/ppermute | solution.py:31
  459.2 14.3 %collective-permute-start.40 = (f32[2,66,384]{2,1,0:T(8,128)S(1)}, f32[2,66,384]{2,1,0:T(8,128)S(1)}, u32[]{:S(2)}, u32[]{:S(2)}) collective-permute-start(f32[2,66,384]{2,1,0:T(8,128)S(1)} %pad_maximum_fusion.51), channel_id=1, source_target_pairs={{64,0},{96,32},{1,65},{33,97},{66,2},{98,34},{3,67},{35,99},{68,4}... | collective-permute-start | bytes 608264 | tf_op jit(solution)/shard_map/ppermute | solution.py:677
  467.9 15.2 %all-to-all-start.4 = ((f32[64,8,128]{2,1,0:T(8,128)}), f32[64,8,128]{2,1,0:T(8,128)S(1)}, u32[]{:S(2)}, u32[]{:S(2)}) async-start(f32[64,8,128]{2,1,0:T(8,128)} %broadcast_in_dim.311), calls=%async_computation.6 | async-start | bytes 524288 | tf_op jit(solution)/shard_map/all_to_all | solution.py:131
  473.5 11.5 %collective-permute-start.41 = (f32[66,768]{1,0:T(8,128)S(1)}, f32[66,768]{1,0:T(8,128)S(1)}, u32[]{:S(2)}, u32[]{:S(2)}) collective-permute-start(f32[66,768]{1,0:T(8,128)S(1)} %select_bitcast_fusion), channel_id=1, source_target_pairs={{0,1},{1,0},{2,3},{3,2},{4,5},{5,4},{6,7},{7,6},{8,9},{9,8},{10,11... | collective-permute-start | bytes 608264 | tf_op jit(solution)/shard_map/ppermute | solution.py:31
  (180 other events, 1227.3 us)
Sparse Core Ops, SparseCore 0:
  41.5 99.3 all-gather.2
  146.2 53.1 all-gather.4
  243.7 75.5 reduce-scatter.4
  327.7 99.3 reduce-scatter.2
